TPU v7x, 256 devices: a whole 4x4x8 slice. The times are simulated.
256 devices in a mesh: ch: 8 (over y, core), seq: 32 (over x, z).
Axes of the slice: x: 4, y: 4, z: 8, core: 2. Of those that a mesh axis runs over, the one named last changes fastest.
Arguments:
- tokens: bfloat16 [24576, 4096], P('seq'), may hold values from -6 to 6
- in_weight: bfloat16 [4096, 3, 4096], P('seq', None, 'ch'), may hold values from -0.09375 to 0.09375
- short_weight: float32 [3, 3, 4096], P(None, None, 'ch'), may hold values from -3 to 3
- decay_rate: float32 [16, 4096], P(None, 'ch'), may hold values from 0 to 1
- residue: float32 [16, 4096], P(None, 'ch'), may hold values from -1.5 to 1.5
- out_weight: bfloat16 [4096, 4096], P('ch'), may hold values from -0.125 to 0.125
- contig_lengths: int32 [16], replicated, may hold values from 1 to 6144, 24576 in all
Outputs:
- mixed: bfloat16 [24576, 4096], P('seq', 'ch')
Inputs may be any that keep to these rules, and one draw needn't show every extreme that they name: `contig_lengths`: the lengths sum to 24576; the largest is exactly 6144.
All inputs are finite; a program needn't handle non-finite values.
Results may differ from a plain program's by a relative error of at most 0.0049.
Values may be sent and summed in bfloat16 or wider, within the bound.
No kernel may reach another device: no remote copies, remote signals or barrier semaphores. Data moves between devices by JAX's collectives and lax.ppermute only.
A program may use at most 128 MiB of HBM per device.

v0:
```python
import jax
import jax.numpy as jnp
from jax import lax
from jax.sharding import PartitionSpec as P

HIGHEST = lax.Precision.HIGHEST


def from_behind(block, axis, distance):
    devices = range(lax.axis_size(axis))
    route = [(i - distance, i) for i in devices if i - distance in devices]
    return lax.ppermute(block, axis, route)


def prefix(value, axis, combine, identity):
    devices, place = (lax.axis_size(axis), lax.axis_index(axis))
    everything = jax.tree.map(lambda part: lax.all_gather(part, axis), value)
    start = jax.tree.map(
        lambda part, zero: jnp.broadcast_to(jnp.asarray(zero, part.dtype), part.shape),
        value,
        identity,
    )

    def hop(k, before):
        reached = k < place
        new = combine(before, jax.tree.map(lambda part: part[k], everything))
        return jax.tree.map(lambda a, b: jnp.where(reached, a, b), new, before)

    return lax.fori_loop(0, devices, hop, start)


def per_device(tokens, in_weight, short_weight, decay_rate, residue, out_weight, contig_lengths):
    tok_rows = tokens.shape[0]
    chan_cols = in_weight.shape[2]
    modes_count = decay_rate.shape[0]
    projected = jnp.einsum(
        "td,dpc->tpc",
        tokens,
        lax.all_gather(in_weight, "seq", axis=0, tiled=True),
        preferred_element_type=jnp.float32,
    )
    shard_at = lax.axis_index("seq")
    starts = jnp.cumsum(contig_lengths) - contig_lengths
    position = shard_at * tok_rows - 1 + jnp.arange(tok_rows + 1, dtype=jnp.int32)
    first_ext = jnp.any(position[:, None] == starts[None, :], axis=1).astype(jnp.int32)
    keep_ext = (1 - first_ext).astype(jnp.float32)
    keep_flag = keep_ext[1:]
    mask_two = keep_flag * keep_ext[:-1]
    prior_rows = from_behind(projected[tok_rows - 2 :], "seq", 1)
    extended = jnp.concatenate([prior_rows, projected], axis=0)
    prev_one = extended[1 : tok_rows + 1]
    prev_two = extended[:tok_rows]
    filtered = (
        short_weight[:, 0][None] * projected
        + keep_flag[:, None, None] * (short_weight[:, 1][None] * prev_one)
        + mask_two[:, None, None] * (short_weight[:, 2][None] * prev_two)
    )
    drive_in = filtered[:, 1] * filtered[:, 2]
    block_len = 64
    block_count = tok_rows // block_len
    coef_mode = residue * jnp.sqrt(-jnp.expm1(-2.0 * decay_rate))
    steps_at = jnp.arange(block_len, dtype=jnp.float32)
    power_now = jnp.exp(-decay_rate[None] * steps_at[:, None, None])
    power_next = jnp.exp(-decay_rate[None] * (steps_at[:, None, None] + 1.0))
    power_tail = jnp.exp(-decay_rate[None] * (block_len - 1.0 - steps_at)[:, None, None])
    kernel_rows = jnp.sum(coef_mode[None] * power_now, axis=1)
    lag_index = (
        jnp.arange(block_len, dtype=jnp.int32)[:, None]
        - jnp.arange(block_len, dtype=jnp.int32)[None, :]
    )
    toeplitz = jnp.where((lag_index >= 0)[:, :, None], kernel_rows[jnp.maximum(lag_index, 0)], 0.0)
    inflow = coef_mode[None] * power_next
    block_decay = jnp.exp(-decay_rate * block_len)
    drive_blocks = drive_in.reshape(block_count, block_len, chan_cols)
    first_blocks = (1.0 - keep_flag).reshape(block_count, block_len)
    counts_in = jnp.cumsum(first_blocks, axis=1)

    def one_block(carried, inputs):
        drive_block, counts = inputs
        same_seg = jnp.where(counts[:, None] == counts[None, :], 1.0, 0.0)
        within = jnp.einsum(
            "tsc,sc->tc", toeplitz * same_seg[:, :, None], drive_block, precision=HIGHEST
        )
        alive_row = jnp.where(counts == 0, 1.0, 0.0)
        inward = alive_row[:, None] * jnp.einsum("tmc,mc->tc", inflow, carried, precision=HIGHEST)
        reach_end = jnp.where(counts == counts[-1], 1.0, 0.0)
        fresh_in = jnp.einsum(
            "smc,sc->mc", power_tail, reach_end[:, None] * drive_block, precision=HIGHEST
        )
        carried = jnp.where(counts[-1] == 0, 1.0, 0.0) * block_decay * carried + fresh_in
        return (carried, within + inward)

    local_state, local_blocks = lax.scan(
        one_block, jnp.zeros((modes_count, chan_cols), jnp.float32), (drive_blocks, counts_in)
    )
    local_long = local_blocks.reshape(tok_rows, chan_cols)
    untouched = jnp.where(jnp.sum(first_blocks) == 0, 1.0, 0.0)
    shard_decay = untouched * jnp.exp(-decay_rate * tok_rows)

    def combine(earlier, later):
        return (earlier[0] * later[0], later[0] * earlier[1] + later[1])

    identity_pair = (jnp.ones_like(shard_decay), jnp.zeros_like(local_state))
    _, incoming = prefix((shard_decay, local_state), "seq", combine, identity_pair)
    alive_shard = jnp.where(jnp.cumsum(1.0 - keep_flag) == 0, 1.0, 0.0)
    block_starts = jnp.arange(block_count, dtype=jnp.float32) * block_len
    entering = jnp.exp(-decay_rate[None] * block_starts[:, None, None]) * incoming[None]
    arriving = jnp.einsum("jmc,kmc->kjc", inflow, entering, precision=HIGHEST).reshape(
        tok_rows, chan_cols
    )
    longconv = local_long + alive_shard[:, None] * arriving
    gated = (filtered[:, 0] * longconv).astype(jnp.bfloat16)
    partial_out = jnp.dot(gated, out_weight, preferred_element_type=jnp.float32)
    mixed = lax.psum_scatter(partial_out, "ch", scatter_dimension=1, tiled=True)
    return mixed.astype(jnp.bfloat16)


def solution(mesh):
    placed = (
        P("seq", None),
        P("seq", None, "ch"),
        P(None, None, "ch"),
        P(None, "ch"),
        P(None, "ch"),
        P("ch", None),
        P(),
    )
    return jax.shard_map(
        per_device, mesh=mesh, in_specs=placed, out_specs=P("seq", "ch"), check_vma=False
    )
```

profile of v0, /device:TPU:2, one launch (start us, length us, event | category | flops | bytes accessed | tf_op | source)
XLA Modules:
  0.0 481.6 jit_solution(3980919474719995637)
XLA Ops:
  13.7 6.0 %multiply_reduce_fusion.3 = f32[64,512]{0,1:T(8,128)S(1)} fusion(f32[16,512]{0,1:T(8,128)S(1)} %copy.28, f32[16,512]{0,1:T(8,128)S(1)} %copy.29), kind=kLoop, calls=%fused_computation.39 | loop fusion | flops 1540096 | bytes 196608 | tf_op jit(solution)/shard_map/reduce_sum | solution.py:66
  19.8 16.8 %gather_fusion = f32[4096,512]{1,0:T(8,128)} fusion(f32[64,512]{1,0:T(8,128)S(1)} %copy.30, s32[4096]{0:T(1024)S(1)} %broadcast_clamp_fusion), kind=kCustom, calls=%fused_computation | custom fusion | bytes 16793600 | tf_op jit(solution)/shard_map/gather | solution.py:71
  36.6 5.8 %broadcast_select_fusion = f32[64,64,512]{2,1,0:T(8,128)} fusion(f32[64,64,512]{2,1,0:T(8,128)} %bitcast.103, pred[64,64]{1,0:T(8,128)(4,1)S(1)} %subtract_compare_fusion), kind=kLoop, calls=%fused_computation.38 | loop fusion | flops 2097152 | bytes 16781312 | tf_op jit(solution)/shard_map/jit(_where)/select_n | solution.py:71
  42.5 88.9 %all-gather.6.cloned.1.call-done = bf16[4096,3,512]{2,0,1:T(8,128)(2,1)} async-done(((bf16[128,3,512]{2,0,1:T(8,128)(2,1)}), bf16[4096,3,512]{2,0,1:T(8,128)(2,1)}) %all-gather.6.cloned.1.call-update) | async-done | bytes 12582928 | tf_op jit(solution)/shard_map/all_gather | solution.py:39
  131.3 13.9 %fusion.6 = f32[768,3,512]{2,0,1:T(8,128)S(1)} fusion(bf16[4096,3,512]{2,0,1:T(8,128)(2,1)} %all-gather.6.cloned.1.call-done, bf16[768,4096]{1,0:T(8,128)(2,1)} %param.11), kind=kOutput, calls=%fused_computation.19 | convolution fusion | flops 9663676416 | bytes 23592960 | tf_op jit(solution)/shard_map/td,dpc->tpc/dot_general | solution.py:36
  155.1 6.2 %fusion.12 = f32[768,3,512]{2,0,1:T(8,128)S(1)} fusion(f32[2,3,512]{2,0,1:T(2,128)S(1)} %collective-permute-done, f32[768,3,512]{2,0,1:T(8,128)} %copy-done.1, f32[3,512]{1,0:T(4,128)S(1)} %get-tuple-element.319, f32[768]{0:T(1024)S(1)} %get-tuple-element.317, f32[3,512]{1,0:T(4,128)S(1)} %get-tuple-element.320, f32[768]{0:T(1024)S(1)} %get-tuple-element.318, ...), kind=kLoop, calls=%fused_computation.27 | loop fusion | flops 10616832 | bytes 9474048 | tf_op jit(solution)/shard_map/add | solution.py:54
  163.8 115.2 %while.30 = (s32[]{:T(128)}, f32[16,512]{1,0:T(8,128)S(1)}, f32[12,64,512]{2,1,0:T(8,128)S(1)}, f32[12,64]{1,0:T(8,128)}, f32[16,512]{1,0:T(8,128)S(1)}, /*index...) while((s32[]{:T(128)}, f32[16,512]{1,0:T(8,128)S(1)}, ...), condition=%wide.region_5.6_spmd.clone.clone.clone, body=%wide.region_4.5_spmd.clone.clone.clone.sunk | while | flops 10027269 | bytes 10193869 | solution.py:93
  168.9 4.3 multiply_reduce_fusion.8
  178.5 4.4 multiply_reduce_fusion.8
  188.2 4.4 multiply_reduce_fusion.8
  197.8 4.4 multiply_reduce_fusion.8
  207.4 4.3 multiply_reduce_fusion.8
  217.0 4.3 multiply_reduce_fusion.8
  226.5 4.3 multiply_reduce_fusion.8
  236.1 4.3 multiply_reduce_fusion.8
  245.7 4.3 multiply_reduce_fusion.8
  255.3 4.3 multiply_reduce_fusion.8
  264.9 4.3 multiply_reduce_fusion.8
  274.5 4.3 multiply_reduce_fusion.8
  280.4 71.9 %all-gather.10.cloned.1.call-done = f32[512,512]{1,0:T(8,128)} async-done(((f32[16,512]{1,0:T(8,128)}), f32[512,512]{1,0:T(8,128)}) %all-gather.10.cloned.1.call-update) | async-done | bytes 1048592 | tf_op jit(solution)/shard_map/all_gather | solution.py:17
  352.3 26.0 %while.29 = (s32[]{:T(128)}, f32[16,512]{1,0:T(8,128)S(1)}, s32[]{:T(128)}, f32[32,16,512]{2,1,0:T(8,128)}, f32[32,16,512]{2,1,0:T(8,128)}, /*index=5*/s32[]{:T(128)}, s32[]{:T(128)}) while((s32[]{:T(128)}, f32[16,512]{1,0:T(8,128)S(1)}, s32[]{:T(128)}, f32[32,16,512]{2,1,0:T(8,128)}, f32[32,16,512]{2,1,0:T(8,128)}, ...), condition=%wide.region_10.11_spmd.clone, body=%wide.region_9.10_spmd.clone.sunk | while | flops 32772 | bytes 131173 | solution.py:29
  378.4 8.5 %fusion.22 = f32[12,64,512]{1,0,2:T(8,128)} fusion(f32[16,512]{0,1:T(8,128)S(1)} %copy.32, f32[12]{0:T(128)S(1)} %iota_multiply_fusion, f32[16,512]{0,1:T(8,128)} %copy-done.3, f32[64]{0:T(128)S(1)} %get-tuple-element.513, f32[16,512]{0,1:T(8,128)S(1)} %copy.28), kind=kOutput, calls=%fused_computation.40 | convolution fusion | flops 76742656 | bytes 1671472 | tf_op jit(solution)/shard_map/jmc,kmc->kjc/dot_general | solution.py:108
  392.6 6.3 %fusion.40 = f32[768,4096]{1,0:T(8,128)} fusion(bf16[768,512]{1,0:T(8,128)(2,1)S(1)} %fusion.34, bf16[512,4096]{1,0:T(8,128)(2,1)S(1)} %copy-done.5), kind=kOutput, calls=%fused_computation.77 | convolution fusion | flops 3221225472 | bytes 17563648 | tf_op jit(solution)/shard_map/dot_general | solution.py:113
  398.9 73.7 %reduce-scatter.2.cloned.1.call-done = f32[768,512]{1,0:T(8,128)} async-done(((f32[768,4096]{1,0:T(8,128)}), f32[768,512]{1,0:T(8,128)}) %reduce-scatter.2.cloned.1.call-update) | async-done | bytes 1572880 | tf_op jit(solution)/shard_map/reduce_scatter | solution.py:114
  (212 shorter events, 109.2 us)
Async XLA Ops:
  6.5 124.8 %all-gather.6.cloned.1.call-start = ((), (), s32[]{:S(2)}) async-start(), calls=%async_computation.1 | async-start | bytes 12976128 | tf_op jit(solution)/shard_map/all_gather | solution.py:39
  7.3 273.1 %all-gather.8.cloned.1.call-start = ((), (), s32[]{:S(2)}) async-start(), calls=%async_computation.3 | async-start | bytes 1081344 | tf_op jit(solution)/shard_map/all_gather | solution.py:17
  11.7 8.0 %copy-start.4 = (f32[16,512]{1,0:T(8,128)}, f32[16,512]{1,0:T(8,128)S(1)}, u32[]{:S(2)}) copy-start(f32[16,512]{1,0:T(8,128)S(1)} %get-tuple-element.439) | copy-start | bytes 98308
  11.7 340.5 %all-gather.10.cloned.1.call-start = ((), (), s32[]{:S(2)}) async-start(), calls=%async_computation.4 | async-start | bytes 1081344 | tf_op jit(solution)/shard_map/all_gather | solution.py:17
  12.9 0.7 copy-start.3
  145.2 2.1 copy-start.1
  147.4 7.7 %collective-permute-start = (f32[2,3,512]{2,0,1:T(2,128)S(1)}, f32[2,3,512]{2,0,1:T(2,128)S(1)}, u32[]{:S(2)}, u32[]{:S(2)}) collective-permute-start(f32[2,3,512]{2,0,1:T(2,128)S(1)} %slice.63), channel_id=1, source_target_pairs={{0,1},{1,2},{2,3},{3,4},{4,5},{5,6},{6,7},{7,8},{8,9},{9,10},{10,1... | collective-permute-start | bytes 36872 | tf_op jit(solution)/shard_map/ppermute | solution.py:12
  161.3 2.1 copy-start
  278.9 0.6 copy-start.2
  279.6 193.1 %reduce-scatter.2.cloned.1.call-start = ((), (), s32[]{:S(2)}) async-start(), calls=%async_computation.2 | async-start | bytes 14155776 | tf_op jit(solution)/shard_map/reduce_scatter | solution.py:114
  389.9 2.7 copy-start.5
Sparse Core Ops, SparseCore 0:
  9.9 121.3 all-gather.5
  133.9 73.4 all-gather.7
  279.7 72.5 all-gather.9
  399.1 73.5 reduce-scatter.1
where the time goes:
time: 486 us; the launch traced here: 482 us
  waiting for transfers between devices  240 us (49%)
  other arithmetic  153 us (31%)
  local copies, waits for them, and re-layouts  35.7 us (7%)
  matrix products  28.7 us (6%)
  between operations  14 us (3%)
  loops' own time  8.38 us (2%)
    all_gather x1, waiting for transfers between devices, per_device(): lax.all_gather(in_weight, 'seq', axis=0, tiled=True)  88.9 us
    reduce_scatter x1, waiting for transfers between devices, per_device(): mixed = lax.psum_scatter(partial_out, 'ch', scatter_dimension=1, tiled=True)  73.7 us
    all_gather x2, waiting for transfers between devices, prefix(): everything = jax.tree.map(lambda part: lax.all_gather(part, axis), value)  71.9 us
    dot_general x12, other arithmetic, one_block(): jnp.einsum('tsc,sc->tc', toeplitz * same_seg[:, :, None], drive_block, pr...  52.1 us
    select_n x32, other arithmetic, hop(): return jax.tree.map(lambda a, b: jnp.where(reached, a, b), new, before)  25.2 us
    dot_general x12, other arithmetic, one_block(): jnp.einsum('tmc,mc->tc', inflow, carried, precision=HIGHEST)  17.5 us
    gather x1, local copies, waits for them, and re-layouts, per_device(): kernel_rows[jnp.maximum(lag_index, 0)]  16.8 us
    dot_general x1, matrix products, per_device(): jnp.einsum('td,dpc->tpc', tokens, lax.all_gather(in_weight, 'seq', axis=0...  13.9 us
  transfers between devices with their start and end apart: 5, of which 4 were waited for; matrix products, arithmetic and copies ran while one was open for 34% of the time, Pallas kernels for 0%

commit v1 on v0

v1 whole, which is shorter than its diff:
```python
import functools
import jax
import jax.numpy as jnp
from jax import lax
from jax.experimental import pallas as pl
from jax.experimental.pallas import tpu as pltpu
from jax.sharding import PartitionSpec as P

F32, BF16 = jnp.float32, jnp.bfloat16
HALO = 16
CHUNKS = 8
LANES = 128


def load_tokens(order, place_ref, tok_hbm, halo_hbm, tok, sem):
    rows = tok_hbm.shape[0]
    copies = [pltpu.make_async_copy(halo_hbm, tok.at[pl.ds(0, HALO)], sem)]
    body = tok.at[pl.ds(HALO, rows)]
    copies.append(pltpu.make_async_copy(tok_hbm, body, sem))
    for c in copies:
        c.start()
    for c in copies:
        c.wait()


def project(tok, pieces, acc, step=1024):
    first = True
    k0 = 0
    for w in pieces:
        depth = w.shape[0]
        size = min(step, depth)
        n = depth // size

        def one(i, k0=k0, w=w, size=size):
            at = pl.multiple_of(k0 + i * size, 128)
            wi = pl.multiple_of(i * size, 128)
            return jnp.dot(tok[:, pl.ds(at, size)], w[pl.ds(wi, size), :], preferred_element_type=F32)

        start = 0
        if first:
            acc[...] = one(0)
            first, start = False, 1

        @pl.loop(start, n)
        def _(i):
            acc[...] += one(i)

        k0 += depth


def short_filter(acc, cols, taps, keep, mask2, r0, rows):
    window = acc[pl.ds(pl.multiple_of(HALO - 8 + r0, 8), rows + 8), cols]
    cur, one, two = window[8:], window[7:-1], window[6:-2]
    return taps[0:1] * cur + keep * (taps[1:2] * one) + mask2 * (taps[2:3] * two)


def drive_kernel(order, block, place_ref, tok_hbm, halo_hbm, *refs):
    n = len(order)
    pieces, refs = refs[:n], refs[n:]
    kw, vw, keep_ref, mask2_ref, tail_ref, thru_ref, d_ref, dchunk_ref = refs[:8]
    u_ref, end_ref, last_ref, tok, acc, sem, drive, ends = refs[8:]

    @pl.when(pl.program_id(0) == 0)
    def _():
        load_tokens(order, place_ref, tok_hbm, halo_hbm, tok, sem)

    project(tok, pieces, acc)
    steps = u_ref.shape[1]
    modes = d_ref.shape[0]
    for s in range(block // LANES):
        kc = pl.ds(s * LANES, LANES)
        vc = pl.ds(block + s * LANES, LANES)

        @pl.loop(0, CHUNKS)
        def _(j):
            r0 = pl.multiple_of(j * steps, 8)
            keep, mask2 = keep_ref[pl.ds(r0, steps), :], mask2_ref[pl.ds(r0, steps), :]
            fk = short_filter(acc, kc, kw[:, kc], keep, mask2, r0, steps)
            fv = short_filter(acc, vc, vw[:, kc], keep, mask2, r0, steps)
            drive[pl.ds(r0, steps), :] = fk * fv

        d = [jnp.broadcast_to(d_ref[pl.ds(m, 1), kc], (CHUNKS, LANES)) for m in range(modes)]

        def step(t, state):
            u = drive[pl.ds(t, CHUNKS, stride=steps), :]
            u_ref[s, t] = u
            u = u * tail_ref[t]
            return tuple(d[m] * state[m] + u for m in range(modes))

        zero = jnp.zeros((CHUNKS, LANES), F32)
        state = lax.fori_loop(0, steps, step, (zero,) * modes, unroll=4)
        for m in range(modes):
            ends[m] = state[m]
        dc = dchunk_ref[:, kc]
        enter = jnp.zeros((modes, LANES), F32)
        for j in range(CHUNKS):
            mine = ends[:, j, :]
            end_ref[:, j, kc] = mine
            enter = dc * (enter * thru_ref[pl.ds(j, 1), :]) + mine
        last_ref[:, kc] = enter


def query_kernel(order, block, place_ref, tok_hbm, halo_hbm, *refs):
    n = len(order)
    pieces, refs = refs[:n], refs[n:]
    qw, keep_ref, mask2_ref, fq_ref, tok, acc, sem = refs

    @pl.when(pl.program_id(0) == 0)
    def _():
        load_tokens(order, place_ref, tok_hbm, halo_hbm, tok, sem)

    project(tok, pieces, acc)
    rows = fq_ref.shape[0]
    steps = rows // CHUNKS
    for s in range(block // LANES):
        c = pl.ds(s * LANES, LANES)

        @pl.loop(0, CHUNKS)
        def _(j):
            r0 = pl.multiple_of(j * steps, 8)
            keep, mask2 = keep_ref[pl.ds(r0, steps), :], mask2_ref[pl.ds(r0, steps), :]
            fq_ref[pl.ds(r0, steps), c] = short_filter(acc, c, qw[:, c], keep, mask2, r0, steps)


def gate_kernel(u_ref, end_ref, enter_ref, fq_ref, keep_ref, thru_ref, d_ref, dchunk_ref, coef_ref, out_ref, states, long):
    rows, block = fq_ref.shape
    steps = rows // CHUNKS
    modes = d_ref.shape[0]
    for s in range(block // LANES):
        c = pl.ds(s * LANES, LANES)
        dc = dchunk_ref[:, c]
        enter = enter_ref[:, c]
        for j in range(CHUNKS):
            states[:, j, :] = enter
            enter = dc * (enter * thru_ref[pl.ds(j, 1), :]) + end_ref[:, j, c]
        d = [jnp.broadcast_to(d_ref[pl.ds(m, 1), c], (CHUNKS, LANES)) for m in range(modes)]
        coef = [jnp.broadcast_to(coef_ref[pl.ds(m, 1), c], (CHUNKS, LANES)) for m in range(modes)]

        def step(t, state):
            at = pl.ds(t, CHUNKS, stride=steps)
            u, keep = u_ref[s, t], keep_ref[t]
            state = tuple(d[m] * (keep * state[m]) + u for m in range(modes))
            terms = [coef[m] * state[m] for m in range(modes)]
            while len(terms) > 1:
                terms = [a + b for a, b in zip(terms[::2], terms[1::2])]
            long[at, :] = terms[0]
            return state

        lax.fori_loop(0, steps, step, tuple(states[m] for m in range(modes)), unroll=2)

        @pl.loop(0, CHUNKS)
        def _(j):
            at = pl.ds(pl.multiple_of(j * steps, 16), steps)
            out_ref[at, c] = (fq_ref[at, c] * long[at, :]).astype(BF16)


def call_drive(place, tokens, halo, pieces, kw, vw, keep, mask2, tail, thru, d, dchunk, order, block):
    rows, width = tokens.shape
    modes, chans = d.shape
    grid = chans // block
    anywhere = pl.BlockSpec(memory_space=pl.ANY)
    fixed = lambda a: pl.BlockSpec(a.shape, lambda b: (0,) * a.ndim)
    per_chan = lambda a: pl.BlockSpec((a.shape[0], block), lambda b: (0, b))
    return pl.pallas_call(
        functools.partial(drive_kernel, order, block),
        grid=(grid,),
        out_shape=[
            jax.ShapeDtypeStruct((chans // LANES, rows // CHUNKS, CHUNKS, LANES), F32),
            jax.ShapeDtypeStruct((modes, CHUNKS, chans), F32),
            jax.ShapeDtypeStruct((modes, chans), F32),
        ],
        in_specs=[pl.BlockSpec(memory_space=pltpu.SMEM), anywhere, anywhere]
        + [pl.BlockSpec((w.shape[0], 2 * block), lambda b: (0, b)) for w in pieces]
        + [per_chan(kw), per_chan(vw), fixed(keep), fixed(mask2), fixed(tail), fixed(thru), per_chan(d), per_chan(dchunk)],
        out_specs=[
            pl.BlockSpec((block // LANES, rows // CHUNKS, CHUNKS, LANES), lambda b: (b, 0, 0, 0)),
            pl.BlockSpec((modes, CHUNKS, block), lambda b: (0, 0, b)),
            pl.BlockSpec((modes, block), lambda b: (0, b)),
        ],
        scratch_shapes=[
            pltpu.VMEM((HALO + rows, width), BF16),
            pltpu.VMEM((HALO + rows, 2 * block), F32),
            pltpu.SemaphoreType.DMA,
            pltpu.VMEM((rows, LANES), F32),
            pltpu.VMEM((modes, CHUNKS, LANES), F32),
        ],
        compiler_params=pltpu.CompilerParams(vmem_limit_bytes=48 * 2**20),
        cost_estimate=pl.CostEstimate(flops=4 * rows * width * chans, bytes_accessed=2 * width * (rows + 2 * chans), transcendentals=0),
        name="drive",
    )(place, tokens, halo, *pieces, kw, vw, keep, mask2, tail, thru, d, dchunk)


def call_query(place, tokens, halo, pieces, qw, keep, mask2, order, block, first=0):
    rows, width = tokens.shape
    chans = qw.shape[1]
    grid = chans // block
    anywhere = pl.BlockSpec(memory_space=pl.ANY)
    fixed = lambda a: pl.BlockSpec(a.shape, lambda b: (0,) * a.ndim)
    return pl.pallas_call(
        functools.partial(query_kernel, order, block),
        grid=(grid,),
        out_shape=jax.ShapeDtypeStruct((rows, chans), F32),
        in_specs=[pl.BlockSpec(memory_space=pltpu.SMEM), anywhere, anywhere]
        + [pl.BlockSpec((w.shape[0], block), lambda b: (0, first + b)) for w in pieces]
        + [pl.BlockSpec((qw.shape[0], block), lambda b: (0, b)), fixed(keep), fixed(mask2)],
        out_specs=pl.BlockSpec((rows, block), lambda b: (0, b)),
        scratch_shapes=[
            pltpu.VMEM((HALO + rows, width), BF16),
            pltpu.VMEM((HALO + rows, block), F32),
            pltpu.SemaphoreType.DMA,
        ],
        compiler_params=pltpu.CompilerParams(vmem_limit_bytes=48 * 2**20),
        cost_estimate=pl.CostEstimate(flops=2 * rows * width * chans, bytes_accessed=2 * width * (rows + chans), transcendentals=0),
        name="query",
    )(place, tokens, halo, *pieces, qw, keep, mask2)


def call_gate(u, ends, enter, fq, keep, thru, d, dchunk, coef, block):
    rows, chans = fq.shape
    modes = d.shape[0]
    fixed = lambda a: pl.BlockSpec(a.shape, lambda b: (0,) * a.ndim)
    per_chan = lambda a: pl.BlockSpec((a.shape[0], block), lambda b: (0, b))
    return pl.pallas_call(
        gate_kernel,
        grid=(chans // block,),
        out_shape=jax.ShapeDtypeStruct((rows, chans), BF16),
        in_specs=[
            pl.BlockSpec((block // LANES, rows // CHUNKS, CHUNKS, LANES), lambda b: (b, 0, 0, 0)),
            pl.BlockSpec((modes, CHUNKS, block), lambda b: (0, 0, b)),
            per_chan(enter), per_chan(fq), fixed(keep), fixed(thru), per_chan(d), per_chan(dchunk), per_chan(coef),
        ],
        out_specs=pl.BlockSpec((rows, block), lambda b: (0, b)),
        scratch_shapes=[pltpu.VMEM((modes, CHUNKS, LANES), F32), pltpu.VMEM((rows, LANES), F32)],
        compiler_params=pltpu.CompilerParams(vmem_limit_bytes=32 * 2**20),
        cost_estimate=pl.CostEstimate(flops=5 * rows * modes * chans, bytes_accessed=10 * rows * chans, transcendentals=0),
        name="gate",
    )(u, ends, enter, fq, keep, thru, d, dchunk, coef)


def flags(contig_lengths, shard_at, rows):
    starts = jnp.cumsum(contig_lengths) - contig_lengths
    base = shard_at * rows
    position = base - 1 + jnp.arange(rows + 1, dtype=jnp.int32)
    first = jnp.any(position[:, None] == starts[None, :], axis=1)
    keep_ext = jnp.where(first, 0.0, 1.0).astype(F32)
    keep = keep_ext[1:]
    mask2 = keep * keep_ext[:-1]
    steps = rows // CHUNKS
    here = position[1:, None]
    chunk_end = base + (jnp.arange(rows, dtype=jnp.int32)[:, None] // steps + 1) * steps
    tail = jnp.where(jnp.any((starts[None] > here) & (starts[None] < chunk_end), axis=1), 0.0, 1.0).astype(F32)
    lo = base + jnp.arange(CHUNKS, dtype=jnp.int32)[:, None] * steps
    thru = jnp.where(jnp.any((starts[None] >= lo) & (starts[None] < lo + steps), axis=1), 0.0, 1.0).astype(F32)
    wide = lambda a: jnp.broadcast_to(a[:, None], (a.shape[0], LANES))
    slots = lambda a: wide(a).reshape(CHUNKS, steps, LANES).transpose(1, 0, 2)
    return starts, wide(keep), wide(mask2), slots(keep), slots(tail), wide(thru)


def send(value, axis, pairs):
    return lax.ppermute(value, axis, pairs)


def shift_up(size, distance):
    return [(i, i + distance) for i in range(size - distance)]


def swap_cores(size):
    return [(i, i ^ 1) for i in range(size)]


def entering_state(last, starts, decay_shard, shard_at, rows, shards, most):
    state = send(last, "seq", shift_up(shards, 1))
    window = 1
    while window * rows < most:
        lo = (shard_at - window) * rows
        thru = jnp.where(jnp.any((starts >= lo) & (starts < shard_at * rows)), 0.0, 1.0)
        state = state + (thru * decay_shard**window) * send(state, "seq", shift_up(shards, window))
        window *= 2
    return state


def sum_over_channels(gated, out_weight, chips, y, core):
    rows = gated.shape[0]
    width = out_weight.shape[1] // (2 * chips)
    way = 1 - 2 * core
    ring = [(2 * i + c, 2 * ((i + 1 - 2 * c) % chips) + c) for i in range(chips) for c in range(2)]
    partials = []
    for k in range(chips - 1, -1, -1):
        mine_at = (2 * ((y + k * way) % chips) + core) * width
        other_at = (2 * ((y - k * way) % chips) + 1 - core) * width
        columns = lambda at: lax.dynamic_slice_in_dim(out_weight, at, width, axis=1)
        other = jnp.dot(gated, columns(other_at), preferred_element_type=F32).astype(BF16)
        partials.append((columns(mine_at), send(other, "ch", swap_cores(2 * chips))))
    total = None
    for mine, other in partials:
        block = jnp.dot(gated, mine, preferred_element_type=F32) + other.astype(F32)
        if total is not None:
            block = block + send(total, "ch", ring).astype(F32)
        total = block.astype(BF16)
    return total


def per_device(tokens, in_weight, short_weight, decay_rate, residue, out_weight, contig_lengths):
    rows, width = tokens.shape
    chans = in_weight.shape[2]
    shards, chips = lax.axis_size("seq"), lax.axis_size("ch") // 2
    shard_at, place_ch = lax.axis_index("seq"), lax.axis_index("ch")
    y, core = place_ch // 2, place_ch % 2
    block = 2 * LANES
    most = 6144

    halo = send(tokens[rows - HALO :], "seq", shift_up(shards, 1))
    grouped = in_weight.reshape(-1, 3, chans // block, block)
    kv = jnp.concatenate([grouped[:, 1], grouped[:, 2]], axis=2).reshape(-1, 2 * chans)
    own = jnp.concatenate([kv, in_weight[:, 0]], axis=1)
    whole = lax.all_gather(own, "seq", axis=0, tiled=True)

    starts, keep, mask2, keep_s, tail, thru = flags(contig_lengths, shard_at, rows)
    coef = residue * jnp.sqrt(-jnp.expm1(-2.0 * decay_rate))
    d = jnp.exp(-decay_rate)
    d_chunk = jnp.exp(-decay_rate * (rows // CHUNKS))
    d_shard = jnp.exp(-decay_rate * rows)
    place = jnp.zeros((2,), jnp.int32)
    kw, vw, qw = short_weight[1], short_weight[2], short_weight[0]
    drive, ends, last = call_drive(place, tokens, halo, [whole], kw, vw, keep, mask2, tail, thru, d, d_chunk, [0], block)
    enter = entering_state(last, starts, d_shard, shard_at, rows, shards, most)
    fq = call_query(place, tokens, halo, [whole], qw, keep, mask2, [0], block, 2 * chans // block)
    gated = call_gate(drive, ends, enter, fq, keep_s, thru, d, d_chunk, coef, block)
    return sum_over_channels(gated, out_weight, chips, y, core)


def solution(mesh):
    placed = (
        P("seq", None),
        P("seq", None, "ch"),
        P(None, None, "ch"),
        P(None, "ch"),
        P(None, "ch"),
        P("ch", None),
        P(),
    )
    return jax.shard_map(
        per_device, mesh=mesh, in_specs=placed, out_specs=P("seq", "ch"), check_vma=False
    )
```

time: 486 us -> 253 us (0.52)
  other arithmetic: 153 us -> 6.81 us
  waiting for transfers between devices: 240 us -> 158 us
  Pallas kernels: 0 us -> 35.1 us
  local copies, waits for them, and re-layouts: 35.7 us -> 4.35 us
  starting transfers between devices: 2.21 us -> 16.7 us
  matrix products: 28.7 us -> 15.8 us
  loops' own time: 8.38 us -> 0 us
    dot_general x36 -> x0, other arithmetic: 82.5 us -> none  [the longest x12 52.1 us: one_block(): jnp.einsum('tsc,sc->tc', toeplitz * same_seg[:, :, None], drive_block, pr...]
    reduce_scatter x1 -> x0, waiting for transfers between devices: 73.7 us -> none  [per_device(): mixed = lax.psum_scatter(partial_out, 'ch', scatter_dimension=1, tiled=True)]
    all_gather x3 -> x1, waiting for transfers between devices: 161 us -> 109 us  [per_device(): whole = lax.all_gather(own, 'seq', axis=0, tiled=True)]
    select_n x70 -> x3, other arithmetic: 47 us -> 0.02 us  [the longest x1 0.01 us: flags(): jnp.where(jnp.any((starts[None] > here) & (starts[None] < chunk_end), axi...]
    ppermute x1 -> x12, waiting for transfers between devices: 4.29 us -> 48.4 us  [send(): return lax.ppermute(value, axis, pairs)]
    pallas_call x0 -> x3, Pallas kernels: none -> 35.1 us  [the longest x1 18.2 us: call_drive(): pl.pallas_call(functools.partial(drive_kernel, order, block), grid=(grid,...]
    gather x1 -> x0, local copies, waits for them, and re-layouts: 16.8 us -> none  [per_device(): kernel_rows[jnp.maximum(lag_index, 0)]]
    ppermute x1 -> x12, starting transfers between devices: 1.91 us -> 16.7 us  [send(): return lax.ppermute(value, axis, pairs)]
  transfers between devices with their start and end apart: 5 -> 13, of which waited for: 4 -> 9; matrix products, arithmetic and copies ran while one was open for 34% -> 8% of each run, Pallas kernels for 0% -> 4%
where the time goes in v1:
time: 253 us; the launch traced here: 252 us
  waiting for transfers between devices  158 us (62%)
  Pallas kernels  35.1 us (14%)
  starting transfers between devices  16.7 us (7%)
  matrix products  15.8 us (6%)
  between operations  15.6 us (6%)
  other arithmetic  6.81 us (3%)
  local copies, waits for them, and re-layouts  4.35 us (2%)
    all_gather x1, waiting for transfers between devices, per_device(): whole = lax.all_gather(own, 'seq', axis=0, tiled=True)  109 us
    ppermute x12, waiting for transfers between devices, send(): return lax.ppermute(value, axis, pairs)  48.4 us
    pallas_call x1, Pallas kernels, call_drive(): pl.pallas_call(functools.partial(drive_kernel, order, block), grid=(grid,...  18.2 us
    ppermute x12, starting transfers between devices, send(): return lax.ppermute(value, axis, pairs)  16.7 us
    pallas_call x1, Pallas kernels, call_query(): pl.pallas_call(functools.partial(query_kernel, order, block), grid=(grid,...  10.3 us
    dot_general x4, matrix products, sum_over_channels(): jnp.dot(gated, columns(other_at), preferred_element_type=F32).astype(BF16)  8.2 us
    dot_general x4, matrix products, sum_over_channels(): block = jnp.dot(gated, mine, preferred_element_type=F32) + other.astype(F32)  7.56 us
    pallas_call x1, Pallas kernels, call_gate(): pl.pallas_call(gate_kernel, grid=(chans // block,), out_shape=jax.ShapeDt...  6.52 us
  transfers between devices with their start and end apart: 13, of which 9 were waited for; matrix products, arithmetic and copies ran while one was open for 8% of the time, Pallas kernels for 4%

profile of v1, /device:TPU:2, one launch (start us, length us, event | category | flops | bytes accessed | tf_op | source)
XLA Modules:
  0.0 252.1 jit_solution(1401497970803485885)
XLA Ops:
  10.8 3.8 %collective-permute-start = (bf16[16,4096]{1,0:T(8,128)(2,1)S(1)}, bf16[16,4096]{1,0:T(8,128)(2,1)S(1)}, u32[]{:S(2)}, u32[]{:S(2)}) collective-permute-start(bf16[16,4096]{1,0:T(8,128)(2,1)S(1)} %slice.30), channel_id=1, source_target_pairs={{0,1},{1,2},{2,3},{3,4},{4,5},{5,6},{6,7},{7,8},{8,9},{9,10},{10,1... | collective-permute-start | bytes 393224 | tf_op jit(solution)/shard_map/ppermute | solution.py:260
  16.5 5.5 %collective-permute-done.halo_hbm = bf16[16,4096]{1,0:T(8,128)(2,1)S(1)} collective-permute-done((bf16[16,4096]{1,0:T(8,128)(2,1)S(1)}, bf16[16,4096]{1,0:T(8,128)(2,1)S(1)}, u32[]{:S(2)}, u32[]{:S(2)}) %collective-permute-start) | collective-permute-done | bytes 131104 | tf_op jit(solution)/shard_map/ppermute | solution.py:260
  22.0 109.4 %all-gather.2.cloned.1.call-done.refs_0_ = bf16[4096,1536]{1,0:T(8,128)(2,1)} async-done(((bf16[128,1536]{1,0:T(8,128)(2,1)}), bf16[4096,1536]{1,0:T(8,128)(2,1)}) %all-gather.2.cloned.1.call-update) | async-done | bytes 12582928 | tf_op jit(solution)/shard_map/all_gather | solution.py:316
  131.8 18.2 %drive.1 = (f32[4,96,8,128]{3,2,1,0:T(8,128)S(1)}, f32[16,8,512]{2,1,0:T(8,128)S(1)}, f32[16,512]{1,0:T(8,128)S(1)}) custom-call(s32[2]{0:T(128)S(1)} %broadcast_2_place_ref.2.place_ref, bf16[768,4096]{1,0:T(8,128)(2,1)} %tok_hbm.3, bf16[16,4096]{1,0:T(8,128)(2,1)S(1)} %collective-permute-done.halo_hbm, ...), custom_call_target="tpu_custom_call" | custom-call | flops 6442450944 | bytes 14680064 | tf_op jit(solution)/shard_map/drive/pallas_call | solution.py:164
  150.0 1.9 collective-permute-start.1
  151.9 6.0 %collective-permute-done.1 = f32[16,512]{1,0:T(8,128)S(1)} collective-permute-done((f32[16,512]{1,0:T(8,128)S(1)}, f32[16,512]{1,0:T(8,128)S(1)}, u32[]{:S(2)}, u32[]{:S(2)}) %collective-permute-start.1) | collective-permute-done | bytes 32800 | tf_op jit(solution)/shard_map/ppermute | solution.py:260
  157.9 1.9 collective-permute-start.2
  160.5 5.3 %collective-permute-done.2 = f32[16,512]{1,0:T(8,128)S(1)} collective-permute-done((f32[16,512]{1,0:T(8,128)S(1)}, f32[16,512]{1,0:T(8,128)S(1)}, u32[]{:S(2)}, u32[]{:S(2)}) %collective-permute-start.2) | collective-permute-done | bytes 32800 | tf_op jit(solution)/shard_map/ppermute | solution.py:260
  165.8 1.9 collective-permute-start.3
  169.2 5.4 %collective-permute-done.3 = f32[16,512]{1,0:T(8,128)S(1)} collective-permute-done((f32[16,512]{1,0:T(8,128)S(1)}, f32[16,512]{1,0:T(8,128)S(1)}, u32[]{:S(2)}, u32[]{:S(2)}) %collective-permute-start.3) | collective-permute-done | bytes 32800 | tf_op jit(solution)/shard_map/ppermute | solution.py:260
  174.7 2.3 collective-permute-start.4
  177.0 10.3 %query.1.fq_ref = f32[768,512]{1,0:T(8,128)S(1)} custom-call(s32[2]{0:T(128)S(1)} %broadcast_2_place_ref.2.place_ref, bf16[768,4096]{1,0:T(8,128)(2,1)} %tok_hbm.3, bf16[16,4096]{1,0:T(8,128)(2,1)S(1)} %collective-permute-done.halo_hbm, bf16[4096,1536]{1,0:T(8,128)(2,1)} %all-gather.2.cloned.1.call-done.refs_0_, f32[3,512]{1,0:T(4,128)S(1)} %get-tuple-element.21.refs_1_, ...), custom_call_target="tpu_custom_call" | custom-call | flops 3221225472 | bytes 10485760 | tf_op jit(solution)/shard_map/query/pallas_call | solution.py:199
  187.4 6.5 %gate.1 = bf16[768,512]{1,0:T(8,128)(2,1)S(1)} custom-call(f32[4,96,8,128]{3,2,1,0:T(8,128)S(1)} %get-tuple-element.8.u_ref, f32[16,8,512]{2,1,0:T(8,128)S(1)} %get-tuple-element.9.end_ref, f32[16,512]{1,0:T(8,128)S(1)} %multiply_add_fusion.enter_ref, f32[768,512]{1,0:T(8,128)S(1)} %query.1.fq_ref, f32[96,8,128]{2,1,0:T(8,128)S(1)} %broadcast_bitcast_fusion.keep_ref, ...), custom_call_target="tpu_custom_call" | custom-call | flops 31457280 | bytes 3932160 | tf_op jit(solution)/shard_map/gate/pallas_call | solution.py:223
  193.9 1.6 convolution_convert_fusion
  195.7 1.6 convolution_convert_fusion.1
  198.0 2.7 %add_convert_fusion.3 = bf16[768,512]{1,0:T(8,128)(2,1)} fusion(bf16[768,512]{1,0:T(8,128)(2,1)} %collective-permute-done.8, bf16[768,512]{1,0:T(8,128)(2,1)S(1)} %gate.1, bf16[512,4096]{1,0:T(8,128)(2,1)} %param.12, s32[]{:T(128)S(6)} %select_n.130), kind=kOutput, calls=%fused_computation.3 | convolution fusion | flops 403832832 | bytes 2883588 | tf_op jit(solution)/shard_map/dot_general | solution.py:296
  202.2 2.5 convolution_convert_fusion.2
  205.9 1.6 fusion.3
  207.5 6.8 %collective-permute-done.9 = bf16[768,512]{1,0:T(8,128)(2,1)} collective-permute-done((bf16[768,512]{1,0:T(8,128)(2,1)}, bf16[768,512]{1,0:T(8,128)(2,1)}, u32[]{:S(2)}, u32[]{:S(2)}) %collective-permute-start.9) | collective-permute-done | bytes 786464 | tf_op jit(solution)/shard_map/ppermute | solution.py:260
  216.2 2.5 convolution_convert_fusion.3
  221.5 7.6 %collective-permute-done.10 = bf16[768,512]{1,0:T(8,128)(2,1)S(1)} collective-permute-done((bf16[768,512]{1,0:T(8,128)(2,1)S(1)}, bf16[768,512]{1,0:T(8,128)(2,1)S(1)}, u32[]{:S(2)}, u32[]{:S(2)}) %collective-permute-start.10) | collective-permute-done | bytes 786464 | tf_op jit(solution)/shard_map/ppermute | solution.py:260
  229.6 1.6 fusion.9
  231.3 11.6 %collective-permute-done.11 = bf16[768,512]{1,0:T(8,128)(2,1)S(1)} collective-permute-done((bf16[768,512]{1,0:T(8,128)(2,1)S(1)}, bf16[768,512]{1,0:T(8,128)(2,1)S(1)}, u32[]{:S(2)}, u32[]{:S(2)}) %collective-permute-start.11) | collective-permute-done | bytes 786464 | tf_op jit(solution)/shard_map/ppermute | solution.py:260
  242.8 2.4 add_convert_fusion
  (62 shorter events, 15.4 us)
Async XLA Ops:
  6.5 124.8 %all-gather.2.cloned.1.call-start = ((), (), s32[]{:S(2)}) async-start(), calls=%async_computation | async-start | bytes 12976128 | tf_op jit(solution)/shard_map/all_gather | solution.py:316
  8.5 6.1 %copy-start.3 = (s32[16]{0:T(128)S(1)}, s32[16]{0:T(128)}, u32[]{:S(2)}) copy-start(s32[16]{0:T(128)} %param.13) | copy-start | bytes 196
  8.6 7.7 %copy-start.2 = (f32[3,3,512]{2,1,0:T(4,128)S(1)}, f32[3,3,512]{2,1,0:T(4,128)}, u32[]{:S(2)}) copy-start(f32[3,3,512]{2,1,0:T(4,128)} %param.9) | copy-start | bytes 55300
  8.6 7.7 %copy-start = (f32[16,512]{1,0:T(8,128)S(1)}, f32[16,512]{1,0:T(8,128)}, u32[]{:S(2)}) copy-start(f32[16,512]{1,0:T(8,128)} %param.10) | copy-start | bytes 98308
  10.8 11.2 %collective-permute-start = (bf16[16,4096]{1,0:T(8,128)(2,1)S(1)}, bf16[16,4096]{1,0:T(8,128)(2,1)S(1)}, u32[]{:S(2)}, u32[]{:S(2)}) collective-permute-start(bf16[16,4096]{1,0:T(8,128)(2,1)S(1)} %slice.30), channel_id=1, source_target_pairs={{0,1},{1,2},{2,3},{3,4},{4,5},{5,6},{6,7},{7,8},{8,9},{9,10},{10,1... | collective-permute-start | bytes 393224 | tf_op jit(solution)/shard_map/ppermute | solution.py:260
  131.7 42.9 %copy-start.1 = (f32[16,512]{1,0:T(8,128)S(1)}, f32[16,512]{1,0:T(8,128)}, u32[]{:S(2)}) copy-start(f32[16,512]{1,0:T(8,128)} %param.11) | copy-start | bytes 98308
  150.0 7.9 %collective-permute-start.1 = (f32[16,512]{1,0:T(8,128)S(1)}, f32[16,512]{1,0:T(8,128)S(1)}, u32[]{:S(2)}, u32[]{:S(2)}) collective-permute-start(f32[16,512]{1,0:T(8,128)S(1)} %get-tuple-element.10), channel_id=1, source_target_pairs={{0,1},{1,2},{2,3},{3,4},{4,5},{5,6},{6,7},{7,8},{8,9},{9,10},{10,1... | collective-permute-start | bytes 98312 | tf_op jit(solution)/shard_map/ppermute | solution.py:260
  157.9 7.9 %collective-permute-start.2 = (f32[16,512]{1,0:T(8,128)S(1)}, f32[16,512]{1,0:T(8,128)S(1)}, u32[]{:S(2)}, u32[]{:S(2)}) collective-permute-start(f32[16,512]{1,0:T(8,128)S(1)} %collective-permute-done.1), channel_id=1, source_target_pairs={{0,1},{1,2},{2,3},{3,4},{4,5},{5,6},{6,7},{7,8},{8,9},{9,10},{10,1... | collective-permute-start | bytes 98312 | tf_op jit(solution)/shard_map/ppermute | solution.py:260
  165.8 8.8 %collective-permute-start.3 = (f32[16,512]{1,0:T(8,128)S(1)}, f32[16,512]{1,0:T(8,128)S(1)}, u32[]{:S(2)}, u32[]{:S(2)}) collective-permute-start(f32[16,512]{1,0:T(8,128)S(1)} %multiply_add_fusion.2), channel_id=1, source_target_pairs={{0,2},{1,3},{2,4},{3,5},{4,6},{5,7},{6,8},{7,9},{8,10},{9,11},{10,... | collective-permute-start | bytes 98312 | tf_op jit(solution)/shard_map/ppermute | solution.py:260
  174.7 12.6 %collective-permute-start.4 = (f32[16,512]{1,0:T(8,128)S(1)}, f32[16,512]{1,0:T(8,128)S(1)}, u32[]{:S(2)}, u32[]{:S(2)}) collective-permute-start(f32[16,512]{1,0:T(8,128)S(1)} %get-tuple-element.18), channel_id=1, source_target_pairs={{0,4},{1,5},{2,6},{3,7},{4,8},{5,9},{6,10},{7,11},{8,12},{9,13},{1... | collective-permute-start | bytes 98312 | tf_op jit(solution)/shard_map/ppermute | solution.py:260
  195.5 2.5 collective-permute-start.8
  197.3 10.2 %collective-permute-start.7 = (bf16[768,512]{1,0:T(8,128)(2,1)S(1)}, bf16[768,512]{1,0:T(8,128)(2,1)S(1)}, u32[]{:S(2)}, u32[]{:S(2)}) collective-permute-start(bf16[768,512]{1,0:T(8,128)(2,1)S(1)} %convolution_convert_fusion.1), channel_id=1, source_target_pairs={{0,32},{32,0},{64,96},{96,64},{128,160},{160,128},{192,224},{224,1... | collective-permute-start | bytes 2359304 | tf_op jit(solution)/shard_map/ppermute | solution.py:260
  200.8 13.5 %collective-permute-start.9 = (bf16[768,512]{1,0:T(8,128)(2,1)}, bf16[768,512]{1,0:T(8,128)(2,1)}, u32[]{:S(2)}, u32[]{:S(2)}) collective-permute-start(bf16[768,512]{1,0:T(8,128)(2,1)} %add_convert_fusion.3), channel_id=1, source_target_pairs={{0,64},{32,224},{64,128},{96,32},{128,192},{160,96},{192,0},{224,1... | collective-permute-start | bytes 2359304 | tf_op jit(solution)/shard_map/ppermute | solution.py:260
  204.7 16.7 %collective-permute-start.6 = (bf16[768,512]{1,0:T(8,128)(2,1)}, bf16[768,512]{1,0:T(8,128)(2,1)S(1)}, u32[]{:S(2)}, u32[]{:S(2)}) collective-permute-start(bf16[768,512]{1,0:T(8,128)(2,1)} %convolution_convert_fusion.2), channel_id=1, source_target_pairs={{0,32},{32,0},{64,96},{96,64},{128,160},{160,128},{192,224},{224,1... | collective-permute-start | bytes 2359304 | tf_op jit(solution)/shard_map/ppermute | solution.py:260
  215.8 13.3 %collective-permute-start.10 = (bf16[768,512]{1,0:T(8,128)(2,1)S(1)}, bf16[768,512]{1,0:T(8,128)(2,1)S(1)}, u32[]{:S(2)}, u32[]{:S(2)}) collective-permute-start(bf16[768,512]{1,0:T(8,128)(2,1)S(1)} %add_convert_fusion.2), channel_id=1, source_target_pairs={{0,64},{32,224},{64,128},{96,32},{128,192},{160,96},{192,0},{224,1... | collective-permute-start | bytes 2359304 | tf_op jit(solution)/shard_map/ppermute | solution.py:260
  218.7 12.6 %collective-permute-start.5 = (bf16[768,512]{1,0:T(8,128)(2,1)}, bf16[768,512]{1,0:T(8,128)(2,1)}, u32[]{:S(2)}, u32[]{:S(2)}) collective-permute-start(bf16[768,512]{1,0:T(8,128)(2,1)} %convolution_convert_fusion.3), channel_id=1, source_target_pairs={{0,32},{32,0},{64,96},{96,64},{128,160},{160,128},{192,224},{224,1... | collective-permute-start | bytes 2359304 | tf_op jit(solution)/shard_map/ppermute | solution.py:260
  229.5 13.3 %collective-permute-start.11 = (bf16[768,512]{1,0:T(8,128)(2,1)S(1)}, bf16[768,512]{1,0:T(8,128)(2,1)S(1)}, u32[]{:S(2)}, u32[]{:S(2)}) collective-permute-start(bf16[768,512]{1,0:T(8,128)(2,1)S(1)} %add_convert_fusion.1), channel_id=1, source_target_pairs={{0,64},{32,224},{64,128},{96,32},{128,192},{160,96},{192,0},{224,1... | collective-permute-start | bytes 2359304 | tf_op jit(solution)/shard_map/ppermute | solution.py:260
Sparse Core Ops, SparseCore 0:
  10.0 121.3 all-gather.1

commit v2 on v1

v2 whole, which is shorter than its diff:
```python
import functools
import jax
import jax.numpy as jnp
from jax import lax
from jax.experimental import pallas as pl
from jax.experimental.pallas import tpu as pltpu
from jax.sharding import PartitionSpec as P

F32, BF16 = jnp.float32, jnp.bfloat16
HALO = 16
CHUNKS = 8
LANES = 128


def tokens_copies(tok_hbm, halo_hbm, tok, sem):
    rows = tok_hbm.shape[0]
    return [
        pltpu.make_async_copy(halo_hbm, tok.at[pl.ds(0, HALO)], sem),
        pltpu.make_async_copy(tok_hbm, tok.at[pl.ds(HALO, rows)], sem),
    ]


def weight_copies(moves, place, sources, weight, depth, cols, sem):
    x, z, core = place[0], place[1], place[2]
    way = 1 - 2 * core
    copies = []
    for source, index, row, rows, dx, dz, half in moves:
        dx = jnp.where(core == 0, dx[0], dx[1]) if isinstance(dx, tuple) else dx
        at = (lax.rem(x + dx * way + 4, 4) * 8 + lax.rem(z + dz * way + 8, 8)) * depth
        if half is not None:
            at = at + (core if half == "own" else 1 - core) * rows
        ref = sources[source]
        for i in index:
            ref = ref.at[i]
        at = pl.multiple_of(at, 16)
        copies.append(
            pltpu.make_async_copy(ref.at[pl.ds(row, rows), cols], weight.at[pl.ds(at, rows)], sem)
        )
    return copies


def project(tok, weight, acc, step=1024):
    def one(i):
        at = pl.multiple_of(i * step, step)
        return jnp.dot(tok[:, pl.ds(at, step)], weight[pl.ds(at, step), :], preferred_element_type=F32)

    acc[...] = one(0)

    @pl.loop(1, weight.shape[0] // step)
    def _(i):
        acc[...] += one(i)


def short_filter(acc, cols, taps, keep, mask2, r0, rows):
    window = acc[pl.ds(pl.multiple_of(HALO - 8 + r0, 8), rows + 8), cols]
    cur, one, two = window[8:], window[7:-1], window[6:-2]
    return taps[0:1] * cur + keep * (taps[1:2] * one) + mask2 * (taps[2:3] * two)


def drive_kernel(moves, block, count, place, tok_hbm, halo_hbm, *refs):
    sources, refs = refs[:count], refs[count:]
    kw, vw, keep_ref, mask2_ref, tail_ref, thru_ref, d_ref, dchunk_ref = refs[:8]
    u_ref, end_ref, last_ref, tok, weights, acc, sem, wsem, drive, ends = refs[8:]
    depth = tok.shape[1] // 32
    steps = u_ref.shape[1]
    modes = d_ref.shape[0]
    blocks = weights.shape[0]

    def copies(b):
        return weight_copies(moves, place, sources, weights.at[b], depth, pl.ds(b * 2 * block, 2 * block), wsem.at[b])

    loads = tokens_copies(tok_hbm, halo_hbm, tok, sem)
    fetch = [copies(b) for b in range(blocks)]
    for c in loads + sum(fetch, []):
        c.start()
    for c in loads:
        c.wait()
    for b in range(blocks):
        for c in fetch[b]:
            c.wait()
        project(tok, weights.at[b], acc)
        for s in range(block // LANES):
            g = b * (block // LANES) + s
            at = pl.ds(g * LANES, LANES)
            kc = pl.ds(s * LANES, LANES)
            vc = pl.ds(block + s * LANES, LANES)

            @pl.loop(0, CHUNKS)
            def _(j):
                r0 = pl.multiple_of(j * steps, 8)
                keep, mask2 = keep_ref[pl.ds(r0, steps), :], mask2_ref[pl.ds(r0, steps), :]
                fk = short_filter(acc, kc, kw[:, at], keep, mask2, r0, steps)
                fv = short_filter(acc, vc, vw[:, at], keep, mask2, r0, steps)
                drive[pl.ds(r0, steps), :] = fk * fv

            d = [jnp.broadcast_to(d_ref[pl.ds(m, 1), at], (CHUNKS, LANES)) for m in range(modes)]

            def step(t, state):
                u = drive[pl.ds(t, CHUNKS, stride=steps), :]
                u_ref[g, t] = u
                u = u * tail_ref[t]
                return tuple(d[m] * state[m] + u for m in range(modes))

            zero = jnp.zeros((CHUNKS, LANES), F32)
            state = lax.fori_loop(0, steps, step, (zero,) * modes, unroll=4)
            for m in range(modes):
                ends[m] = state[m]
            dc = dchunk_ref[:, at]
            enter = jnp.zeros((modes, LANES), F32)
            for j in range(CHUNKS):
                mine = ends[:, j, :]
                end_ref[:, j, at] = mine
                enter = dc * (enter * thru_ref[pl.ds(j, 1), :]) + mine
            last_ref[:, at] = enter


def query_kernel(moves, count, place, tok_hbm, halo_hbm, *refs):
    sources, refs = refs[:count], refs[count:]
    qw, keep_ref, mask2_ref, fq_ref, tok, weight, acc, sem, wsem = refs
    depth = tok.shape[1] // 32
    copies = tokens_copies(tok_hbm, halo_hbm, tok, sem)
    copies += weight_copies(moves, place, sources, weight, depth, slice(None), wsem)
    for c in copies:
        c.start()
    for c in copies:
        c.wait()
    project(tok, weight, acc)
    rows, chans = fq_ref.shape
    steps = rows // CHUNKS
    for s in range(chans // LANES):
        c = pl.ds(s * LANES, LANES)

        @pl.loop(0, CHUNKS)
        def _(j):
            r0 = pl.multiple_of(j * steps, 8)
            keep, mask2 = keep_ref[pl.ds(r0, steps), :], mask2_ref[pl.ds(r0, steps), :]
            fq_ref[pl.ds(r0, steps), c] = short_filter(acc, c, qw[:, c], keep, mask2, r0, steps)


def gate_kernel(u_ref, end_ref, enter_ref, fq_ref, keep_ref, thru_ref, d_ref, dchunk_ref, coef_ref, out_ref, states, long):
    rows, block = fq_ref.shape
    steps = rows // CHUNKS
    modes = d_ref.shape[0]
    for s in range(block // LANES):
        c = pl.ds(s * LANES, LANES)
        dc = dchunk_ref[:, c]
        enter = enter_ref[:, c]
        for j in range(CHUNKS):
            states[:, j, :] = enter
            enter = dc * (enter * thru_ref[pl.ds(j, 1), :]) + end_ref[:, j, c]
        d = [jnp.broadcast_to(d_ref[pl.ds(m, 1), c], (CHUNKS, LANES)) for m in range(modes)]
        coef = [jnp.broadcast_to(coef_ref[pl.ds(m, 1), c], (CHUNKS, LANES)) for m in range(modes)]

        def step(t, state):
            at = pl.ds(t, CHUNKS, stride=steps)
            u, keep = u_ref[s, t], keep_ref[t]
            state = tuple(d[m] * (keep * state[m]) + u for m in range(modes))
            terms = [coef[m] * state[m] for m in range(modes)]
            while len(terms) > 1:
                terms = [a + b for a, b in zip(terms[::2], terms[1::2])]
            long[at, :] = terms[0]
            return state

        lax.fori_loop(0, steps, step, tuple(states[m] for m in range(modes)), unroll=2)

        @pl.loop(0, CHUNKS)
        def _(j):
            at = pl.ds(pl.multiple_of(j * steps, 16), steps)
            out_ref[at, c] = (fq_ref[at, c] * long[at, :]).astype(BF16)


ANYWHERE = pl.BlockSpec(memory_space=pl.ANY)
IN_VMEM = pl.BlockSpec(memory_space=pltpu.VMEM)
IN_SMEM = pl.BlockSpec(memory_space=pltpu.SMEM)


def call_drive(place, tokens, halo, sources, moves, kw, vw, keep, mask2, tail, thru, d, dchunk, block):
    rows, width = tokens.shape
    modes, chans = d.shape
    blocks = chans // block
    return pl.pallas_call(
        functools.partial(drive_kernel, moves, block, len(sources)),
        out_shape=[
            jax.ShapeDtypeStruct((chans // LANES, rows // CHUNKS, CHUNKS, LANES), F32),
            jax.ShapeDtypeStruct((modes, CHUNKS, chans), F32),
            jax.ShapeDtypeStruct((modes, chans), F32),
        ],
        in_specs=[IN_SMEM, ANYWHERE, ANYWHERE] + [ANYWHERE] * len(sources) + [IN_VMEM] * 8,
        out_specs=[IN_VMEM] * 3,
        scratch_shapes=[
            pltpu.VMEM((HALO + rows, width), BF16),
            pltpu.VMEM((blocks, width, 2 * block), BF16),
            pltpu.VMEM((HALO + rows, 2 * block), F32),
            pltpu.SemaphoreType.DMA,
            pltpu.SemaphoreType.DMA((blocks,)),
            pltpu.VMEM((rows, LANES), F32),
            pltpu.VMEM((modes, CHUNKS, LANES), F32),
        ],
        compiler_params=pltpu.CompilerParams(vmem_limit_bytes=40 * 2**20),
        cost_estimate=pl.CostEstimate(flops=8 * rows * width * chans, bytes_accessed=2 * width * (rows + 2 * chans), transcendentals=0),
        name="drive",
    )(place, tokens, halo, *sources, kw, vw, keep, mask2, tail, thru, d, dchunk)


def call_query(place, tokens, halo, sources, moves, qw, keep, mask2):
    rows, width = tokens.shape
    chans = qw.shape[1]
    return pl.pallas_call(
        functools.partial(query_kernel, moves, len(sources)),
        out_shape=jax.ShapeDtypeStruct((rows, chans), F32),
        in_specs=[IN_SMEM, ANYWHERE, ANYWHERE] + [ANYWHERE] * len(sources) + [IN_VMEM] * 3,
        out_specs=IN_VMEM,
        scratch_shapes=[
            pltpu.VMEM((HALO + rows, width), BF16),
            pltpu.VMEM((width, chans), BF16),
            pltpu.VMEM((HALO + rows, chans), F32),
            pltpu.SemaphoreType.DMA,
            pltpu.SemaphoreType.DMA,
        ],
        compiler_params=pltpu.CompilerParams(vmem_limit_bytes=40 * 2**20),
        cost_estimate=pl.CostEstimate(flops=4 * rows * width * chans, bytes_accessed=2 * width * (rows + chans), transcendentals=0),
        name="query",
    )(place, tokens, halo, *sources, qw, keep, mask2)


def call_gate(u, ends, enter, fq, keep, thru, d, dchunk, coef, block):
    rows, chans = fq.shape
    modes = d.shape[0]
    fixed = lambda a: pl.BlockSpec(a.shape, lambda b: (0,) * a.ndim)
    per_chan = lambda a: pl.BlockSpec((a.shape[0], block), lambda b: (0, b))
    return pl.pallas_call(
        gate_kernel,
        grid=(chans // block,),
        out_shape=jax.ShapeDtypeStruct((rows, chans), BF16),
        in_specs=[
            pl.BlockSpec((block // LANES, rows // CHUNKS, CHUNKS, LANES), lambda b: (b, 0, 0, 0)),
            pl.BlockSpec((modes, CHUNKS, block), lambda b: (0, 0, b)),
            per_chan(enter), per_chan(fq), fixed(keep), fixed(thru), per_chan(d), per_chan(dchunk), per_chan(coef),
        ],
        out_specs=pl.BlockSpec((rows, block), lambda b: (0, b)),
        scratch_shapes=[pltpu.VMEM((modes, CHUNKS, LANES), F32), pltpu.VMEM((rows, LANES), F32)],
        compiler_params=pltpu.CompilerParams(vmem_limit_bytes=32 * 2**20),
        cost_estimate=pl.CostEstimate(flops=5 * rows * modes * chans, bytes_accessed=10 * rows * chans, transcendentals=0),
        name="gate",
    )(u, ends, enter, fq, keep, thru, d, dchunk, coef)


def flags(contig_lengths, shard_at, rows):
    starts = jnp.cumsum(contig_lengths) - contig_lengths
    base = shard_at * rows
    position = base - 1 + jnp.arange(rows + 1, dtype=jnp.int32)
    first = jnp.any(position[:, None] == starts[None, :], axis=1)
    keep_ext = jnp.where(first, 0.0, 1.0).astype(F32)
    keep = keep_ext[1:]
    mask2 = keep * keep_ext[:-1]
    steps = rows // CHUNKS
    here = position[1:, None]
    chunk_end = base + (jnp.arange(rows, dtype=jnp.int32)[:, None] // steps + 1) * steps
    tail = jnp.where(jnp.any((starts[None] > here) & (starts[None] < chunk_end), axis=1), 0.0, 1.0).astype(F32)
    lo = base + jnp.arange(CHUNKS, dtype=jnp.int32)[:, None] * steps
    thru = jnp.where(jnp.any((starts[None] >= lo) & (starts[None] < lo + steps), axis=1), 0.0, 1.0).astype(F32)
    wide = lambda a: jnp.broadcast_to(a[:, None], (a.shape[0], LANES))
    slots = lambda a: wide(a).reshape(CHUNKS, steps, LANES).transpose(1, 0, 2)
    return starts, wide(keep), wide(mask2), slots(keep), slots(tail), wide(thru)


def mix_kernel(place, own, theirs, near, far, mid_own, mid_other, w_mine, w_theirs, out_ref):
    core = place[2]
    half = out_ref.shape[0] // 2
    near_at = jnp.where(core == 0, 1, 3)
    far_at = 4 - near_at
    dot = functools.partial(jnp.dot, preferred_element_type=F32)

    @pl.loop(0, 2)
    def _(i):
        rows = pl.ds(pl.multiple_of(i * half, 16), half)
        total = dot(own[rows, :], w_mine[0]) + dot(theirs[rows, :], w_theirs[0])
        total += dot(near[0, rows, :], w_mine[near_at]) + dot(near[1, rows, :], w_theirs[near_at])
        total += dot(far[1, rows, :], w_mine[far_at]) + dot(far[0, rows, :], w_theirs[far_at])
        mine = jnp.where(i == core, mid_own[0], mid_other[1])
        other = jnp.where(i == core, mid_own[1], mid_other[0])
        total += dot(mine, w_mine[2]) + dot(other, w_theirs[2])
        out_ref[rows, :] = total.astype(BF16)


def call_mix(place, own, theirs, near, far, mid_own, mid_other, w_mine, w_theirs):
    rows, chans = own.shape
    width = w_mine.shape[2]
    return pl.pallas_call(
        mix_kernel,
        out_shape=jax.ShapeDtypeStruct((rows, width), BF16),
        in_specs=[IN_SMEM] + [IN_VMEM] * 8,
        out_specs=IN_VMEM,
        compiler_params=pltpu.CompilerParams(vmem_limit_bytes=40 * 2**20),
        cost_estimate=pl.CostEstimate(flops=16 * rows * chans * width, bytes_accessed=16 * rows * chans + 16 * chans * width, transcendentals=0),
        name="mix",
    )(place, own, theirs, near, far, mid_own, mid_other, w_mine, w_theirs)


def send(value, axis, pairs):
    return lax.ppermute(value, axis, pairs)


def shift_up(size, distance):
    return [(i, i + distance) for i in range(size - distance)]


class Routes:
    def __init__(self, chips, xs, zs):
        self.cores = [(i, i ^ 1) for i in range(2 * chips)]
        shards = xs * zs
        self.x, self.z = [], []
        for ch in range(2 * chips):
            way = 1 - 2 * (ch % 2)
            for x in range(xs):
                for z in range(zs):
                    here = ch * shards + x * zs + z
                    self.x.append((here, ch * shards + (x + way) % xs * zs + z))
                    self.z.append((here, ch * shards + x * zs + (z + way) % zs))
        self.y = [(2 * i + c, 2 * ((i + 1 - 2 * c) % chips) + c) for i in range(chips) for c in range(2)]
        self.across = [[(2 * i + c, 2 * ((i + k) % chips) + c) for i in range(chips) for c in range(2)] for k in range(chips)]

    def swap(self, v):
        return send(v, "ch", self.cores)

    def along_x(self, v):
        return send(v, ("ch", "seq"), self.x)

    def along_z(self, v):
        return send(v, ("ch", "seq"), self.z)

    def along_y(self, v):
        return send(v, "ch", self.y)


def joined(core, own, other, axis):
    return jnp.where(core == 0, jnp.concatenate([own, other], axis), jnp.concatenate([other, own], axis))


def half_of(core, value):
    half = value.shape[1] // 2
    return lax.dynamic_slice_in_dim(value, core * half, half, axis=1)


def gather_rows_first(routes, core, mine):
    depth = mine.shape[0]
    chip = jnp.stack([mine, routes.swap(mine)])
    z1, x1 = routes.along_z(chip), routes.along_x(chip)
    z2 = routes.along_z(z1)
    xh = routes.along_x(half_of(core, x1))
    o1 = routes.swap(z1)
    opposite = joined(core, xh, routes.swap(xh)[::-1], 1)
    n1 = routes.along_x(jnp.concatenate([z1, o1[::-1]], 1))
    z3 = routes.along_z(z2)
    f1 = routes.along_z(opposite)
    o2 = routes.swap(z2)
    n2 = routes.along_x(jnp.concatenate([z2, o2[::-1]], 1))
    z4 = routes.along_z(half_of(core, z3))
    f2 = routes.along_z(f1)
    o3 = routes.swap(jnp.concatenate([z3, z4], 1))
    across = joined(core, z4, o3[::-1, depth:], 1)
    n3 = routes.along_x(jnp.concatenate([z3, o3[::-1, :depth], across], 1))
    f3 = routes.along_z(f2)
    f4 = routes.along_z(half_of(core, f3))
    of = routes.swap(jnp.concatenate([f1[1], f2[1], f3[1], f4[1]], 0))
    on = routes.swap(jnp.concatenate([x1[1], n1[1], n2[1]], 0))
    on3 = routes.swap(n3[1])
    sources = [mine, z1, o1, z2, o2, z3, o3, z4, x1, n1, n2, n3, opposite, f1, f2, f3, f4, of, on, on3]
    moves = [(0, (), 0, depth, 0, 0, None)]
    for k, (own, other) in enumerate([(1, 2), (3, 4), (5, 6)], 1):
        moves += [(own, (0,), 0, depth, 0, -k, None), (other, (1,), 0, depth, 0, k, None)]
    moves += [(7, (0,), 0, depth // 2, 0, 4, "own"), (6, (1,), depth, depth // 2, 0, 4, "other")]
    moves += [(8, (0,), 0, depth, -1, 0, None), (18, (), 0, depth, 1, 0, None)]
    for k in (1, 2):
        for i, dz in enumerate((-k, k)):
            moves.append((8 + k, (0,), i * depth, depth, -1, dz, None))
            moves.append((18, (), (2 * k - 1 + i) * depth, depth, 1, -dz, None))
    for i, dz in enumerate((-3, 3, 4)):
        moves.append((11, (0,), i * depth, depth, -1, dz, None))
        moves.append((19, (), i * depth, depth, 1, -dz, None))
    moves.append((12, (0,), 0, depth, 2, 0, None))
    for k in (1, 2, 3):
        moves += [(12 + k, (0,), 0, depth, 2, -k, None), (17, (), (k - 1) * depth, depth, 2, k, None)]
    moves += [(16, (0,), 0, depth // 2, 2, 4, "own"), (17, (), 3 * depth, depth // 2, 2, 4, "other")]
    return sources, moves


def gather_x_first(routes, core, mine):
    depth = mine.shape[0]
    chip = jnp.stack([mine, routes.swap(mine)])
    x1 = routes.along_x(chip)
    xh = routes.along_x(half_of(core, x1))
    o = routes.swap(jnp.concatenate([x1, xh], 1))
    opposite = joined(core, xh, o[::-1, depth:], 1)
    four = jnp.concatenate([chip, x1, opposite, o[::-1, :depth]], 1)
    z1 = routes.along_z(four)
    z2 = routes.along_z(z1)
    z3 = routes.along_z(z2)
    z4 = routes.along_z(lax.dynamic_slice_in_dim(z3, core * depth, 2 * depth, axis=1))
    oz = routes.swap(jnp.concatenate([z1[1], z2[1], z3[1], z4[1]], 0))
    sources = [four, z1, z2, z3, z4, oz]
    moves = []
    for i, dx in enumerate((0, -1, 2, 1)):
        moves.append((0, (0,), i * depth, depth, dx, 0, None))
        for k in (1, 2, 3):
            moves.append((k, (0,), i * depth, depth, dx, -k, None))
            moves.append((5, (), (4 * (k - 1) + i) * depth, depth, -dx, k, None))
    for i, (here, there) in enumerate([((0, -1), (1, 0)), ((-1, 2), (2, 1))]):
        moves.append((4, (0,), i * depth, depth, here, 4, None))
        moves.append((5, (), (12 + i) * depth, depth, there, 4, None))
    return sources, moves


def own_columns(routes, out_weight, chips, y, core):
    width = out_weight.shape[1] // chips
    parts = []
    for k in range(chips):
        block = lax.dynamic_slice_in_dim(out_weight, (y + k) % chips * width, width, axis=1)
        parts.append(block if k == 0 else send(block, "ch", routes.across[k]))
    parts = jnp.stack(parts)
    half = width // 2
    mine = lax.dynamic_slice_in_dim(parts, core * half, half, axis=2)
    other = lax.dynamic_slice_in_dim(parts, (1 - core) * half, half, axis=2)
    return mine, routes.swap(other)


def entering_state(last, starts, decay_shard, shard_at, rows, shards, most):
    state = send(last, "seq", shift_up(shards, 1))
    window = 1
    while window * rows < most:
        lo = (shard_at - window) * rows
        thru = jnp.where(jnp.any((starts >= lo) & (starts < shard_at * rows)), 0.0, 1.0)
        state = state + (thru * decay_shard**window) * send(state, "seq", shift_up(shards, window))
        window *= 2
    return state


def per_device(xs, zs, tokens, in_weight, short_weight, decay_rate, residue, out_weight, contig_lengths):
    rows, width = tokens.shape
    chans = in_weight.shape[2]
    shards, chips = lax.axis_size("seq"), lax.axis_size("ch") // 2
    shard_at, place_ch = lax.axis_index("seq"), lax.axis_index("ch")
    y, core = place_ch // 2, place_ch % 2
    block = 2 * LANES
    most = 6144
    routes = Routes(chips, xs, zs)
    place = jnp.stack([shard_at // zs, shard_at % zs, core]).astype(jnp.int32)

    grouped = in_weight.reshape(-1, 3, chans // block, block)
    kv = jnp.concatenate([grouped[:, 1], grouped[:, 2]], axis=2).reshape(-1, 2 * chans)
    kv_sources, kv_moves = gather_rows_first(routes, core, kv)
    q_sources, q_moves = gather_x_first(routes, core, in_weight[:, 0])
    halo = send(tokens[rows - HALO :], "seq", shift_up(shards, 1))
    w_mine, w_theirs = own_columns(routes, out_weight, chips, y, core)

    starts, keep, mask2, keep_s, tail, thru = flags(contig_lengths, shard_at, rows)
    coef = residue * jnp.sqrt(-jnp.expm1(-2.0 * decay_rate))
    d = jnp.exp(-decay_rate)
    d_chunk = jnp.exp(-decay_rate * (rows // CHUNKS))
    d_shard = jnp.exp(-decay_rate * rows)
    kw, vw, qw = short_weight[1], short_weight[2], short_weight[0]
    drive, ends, last = call_drive(place, tokens, halo, kv_sources, kv_moves, kw, vw, keep, mask2, tail, thru, d, d_chunk, block)
    enter = entering_state(last, starts, d_shard, shard_at, rows, shards, most)
    fq = call_query(place, tokens, halo, q_sources, q_moves, qw, keep, mask2)
    gated = call_gate(drive, ends, enter, fq, keep_s, thru, d, d_chunk, coef, block)

    theirs = routes.swap(gated)
    near = routes.along_y(jnp.stack([gated, theirs]))
    mid = routes.along_y(half_of(core, near))
    far = routes.swap(near)
    mid_other = routes.swap(mid)
    return call_mix(place, gated, theirs, near, far, mid, mid_other, w_mine, w_theirs)


def solution(mesh):
    placed = (
        P("seq", None),
        P("seq", None, "ch"),
        P(None, None, "ch"),
        P(None, "ch"),
        P(None, "ch"),
        P("ch", None),
        P(),
    )
    return jax.shard_map(
        functools.partial(per_device, 4, 8), mesh=mesh, in_specs=placed, out_specs=P("seq", "ch"), check_vma=False
    )
```

time: 253 us -> 305 us (1.21); the launches traced: 252 us -> 300 us
  starting transfers between devices: 16.7 us -> 49.7 us
  local copies, waits for them, and re-layouts: 4.35 us -> 36.8 us
  matrix products: 15.8 us -> 0 us
  other arithmetic: 6.81 us -> 20.2 us
  between operations: 15.6 us -> 3.15 us
  waiting for transfers between devices: 158 us -> 150 us
  Pallas kernels: 35.1 us -> 40 us
    all_gather x1 -> x0, waiting for transfers between devices: 109 us -> none  [per_device(): whole = lax.all_gather(own, 'seq', axis=0, tiled=True)]
    ppermute x12 -> x44, waiting for transfers between devices: 48.4 us -> 150 us  [send(): return lax.ppermute(value, axis, pairs)]
    ppermute x12 -> x44, starting transfers between devices: 16.7 us -> 49.7 us  [send(): return lax.ppermute(value, axis, pairs)]
    dot_general x8 -> x0, matrix products: 15.8 us -> none  [the longest x4 8.2 us: sum_over_channels(): jnp.dot(gated, columns(other_at), preferred_element_type=F32).astype(BF16)]
    squeeze x1 -> x12, local copies, waits for them, and re-layouts: 0.91 us -> 9.5 us  [the longest x4 3.6 us: gather_rows_first(): of = routes.swap(jnp.concatenate([f1[1], f2[1], f3[1], f4[1]], 0))]
    concatenate x1 -> x9, other arithmetic: 0.77 us -> 9.19 us  [the longest x1 2.28 us: gather_rows_first(): n1 = routes.along_x(jnp.concatenate([z1, o1[::-1]], 1))]
    unnamed x9 -> x75, local copies, waits for them, and re-layouts: 0.05 us -> 5.81 us
    rev x0 -> x7, local copies, waits for them, and re-layouts: none -> 5.17 us  [the longest x1 1.08 us: gather_rows_first(): n2 = routes.along_x(jnp.concatenate([z2, o2[::-1]], 1))]
  transfers between devices with their start and end apart: 13 -> 44, of which waited for: 9 -> 20; matrix products, arithmetic and copies ran while one was open for 8% -> 17% of each run, Pallas kernels for 4% -> 6%
where the time goes in v2:
time: 305 us; the launch traced here: 300 us
  waiting for transfers between devices  150 us (49%)
  starting transfers between devices  49.7 us (16%)
  Pallas kernels  40 us (13%)
  local copies, waits for them, and re-layouts  36.8 us (12%)
  other arithmetic  20.2 us (7%)
  between operations  3.15 us (1%)
    ppermute x44, waiting for transfers between devices, send(): return lax.ppermute(value, axis, pairs)  150 us
    ppermute x44, starting transfers between devices, send(): return lax.ppermute(value, axis, pairs)  49.7 us
    pallas_call x1, Pallas kernels, call_drive(): pl.pallas_call(functools.partial(drive_kernel, moves, block, len(sources)...  17.8 us
    pallas_call x1, Pallas kernels, call_query(): pl.pallas_call(functools.partial(query_kernel, moves, len(sources)), out_...  9.21 us
    pallas_call x1, Pallas kernels, call_mix(): pl.pallas_call(mix_kernel, out_shape=jax.ShapeDtypeStruct((rows, width),...  6.54 us
    pallas_call x1, Pallas kernels, call_gate(): pl.pallas_call(gate_kernel, grid=(chans // block,), out_shape=jax.ShapeDt...  6.52 us
  transfers between devices with their start and end apart: 44, of which 20 were waited for; matrix products, arithmetic and copies ran while one was open for 17% of the time, Pallas kernels for 6%

profile of v2, /device:TPU:2, one launch (start us, length us, event | category | flops | bytes accessed | tf_op | source)
XLA Modules:
  0.0 300.0 jit_solution(16939829913619191106)
XLA Ops:
  13.8 6.8 %collective-permute-done.2.refs_1_ = bf16[2,128,1024]{2,1,0:T(8,128)(2,1)} collective-permute-done((bf16[2,128,1024]{2,1,0:T(8,128)(2,1)S(1)}, bf16[2,128,1024]{2,1,0:T(8,128)(2,1)}, u32[]{:S(2)}, u32[]{:S(2)}) %collective-permute-start.2) | collective-permute-done | bytes 524320 | tf_op jit(solution)/shard_map/ppermute | solution.py:301
  24.2 7.0 %collective-permute-done.4.refs_3_ = bf16[2,128,1024]{2,1,0:T(8,128)(2,1)} collective-permute-done((bf16[2,128,1024]{2,1,0:T(8,128)(2,1)}, bf16[2,128,1024]{2,1,0:T(8,128)(2,1)}, u32[]{:S(2)}, u32[]{:S(2)}) %collective-permute-start.4) | collective-permute-done | bytes 524320 | tf_op jit(solution)/shard_map/ppermute | solution.py:301
  38.1 3.7 %collective-permute-done.6.refs_5_ = bf16[2,128,1024]{2,1,0:T(8,128)(2,1)S(1)} collective-permute-done((bf16[2,128,1024]{2,1,0:T(8,128)(2,1)}, bf16[2,128,1024]{2,1,0:T(8,128)(2,1)S(1)}, u32[]{:S(2)}, u32[]{:S(2)}) %collective-permute-start.6) | collective-permute-done | bytes 524320 | tf_op jit(solution)/shard_map/ppermute | solution.py:301
  44.6 2.7 collective-permute-start.15
  58.7 3.0 collective-permute-done.15.refs_13_
  85.2 6.9 %collective-permute-done.17.refs_15_ = bf16[2,128,1024]{2,1,0:T(8,128)(2,1)} collective-permute-done((bf16[2,128,1024]{2,1,0:T(8,128)(2,1)}, bf16[2,128,1024]{2,1,0:T(8,128)(2,1)}, u32[]{:S(2)}, u32[]{:S(2)}) %collective-permute-start.17) | collective-permute-done | bytes 524320 | tf_op jit(solution)/shard_map/ppermute | solution.py:301
  95.4 10.6 %collective-permute-done.18.refs_16_ = bf16[2,64,1024]{2,1,0:T(8,128)(2,1)S(1)} collective-permute-done((bf16[2,64,1024]{2,1,0:T(8,128)(2,1)S(1)}, bf16[2,64,1024]{2,1,0:T(8,128)(2,1)S(1)}, u32[]{:S(2)}, u32[]{:S(2)}) %collective-permute-start.18) | collective-permute-done | bytes 262176 | tf_op jit(solution)/shard_map/ppermute | solution.py:301
  108.1 8.6 %collective-permute-done.33.refs_4_ = bf16[2,256,512]{2,1,0:T(8,128)(2,1)S(1)} collective-permute-done((bf16[2,256,512]{2,1,0:T(8,128)(2,1)S(1)}, bf16[2,256,512]{2,1,0:T(8,128)(2,1)S(1)}, u32[]{:S(2)}, u32[]{:S(2)}) %collective-permute-start.33) | collective-permute-done | bytes 524320 | tf_op jit(solution)/shard_map/ppermute | solution.py:301
  119.0 9.8 %collective-permute-start.34 = (bf16[1792,512]{1,0:T(8,128)(2,1)}, bf16[1792,512]{1,0:T(8,128)(2,1)}, u32[]{:S(2)}, u32[]{:S(2)}) collective-permute-start(bf16[1792,512]{1,0:T(8,128)(2,1)} %pad_maximum_fusion.1), channel_id=1, source_target_pairs={{0,32},{32,0},{64,96},{96,64},{128,160},{160,128},{192,224},{224,1... | collective-permute-start | bytes 5505032 | tf_op jit(solution)/shard_map/ppermute | solution.py:301
  129.3 17.8 %drive.1 = (f32[4,96,8,128]{3,2,1,0:T(8,128)}, f32[16,8,512]{2,1,0:T(8,128)S(1)}, f32[16,512]{1,0:T(8,128)S(1)}) custom-call(s32[3]{0:T(128)S(1)} %pad_add_fusion.place, bf16[768,4096]{1,0:T(8,128)(2,1)} %tok_hbm.3, bf16[16,4096]{1,0:T(8,128)(2,1)} %collective-permute-done.halo_hbm, bf16[128,1024]{1,0:T(8,128)(2,1)S(1)} %bitcast.62, ...), custom_call_target="tpu_custom_call" | custom-call | flops 12884901888 | bytes 14680064 | tf_op jit(solution)/shard_map/drive/pallas_call | solution.py:181
  149.7 6.0 %collective-permute-done.22 = f32[16,512]{1,0:T(8,128)S(1)} collective-permute-done((f32[16,512]{1,0:T(8,128)S(1)}, f32[16,512]{1,0:T(8,128)S(1)}, u32[]{:S(2)}, u32[]{:S(2)}) %collective-permute-start.22) | collective-permute-done | bytes 32800 | tf_op jit(solution)/shard_map/ppermute | solution.py:301
  158.3 5.3 %collective-permute-done.23 = f32[16,512]{1,0:T(8,128)S(1)} collective-permute-done((f32[16,512]{1,0:T(8,128)S(1)}, f32[16,512]{1,0:T(8,128)S(1)}, u32[]{:S(2)}, u32[]{:S(2)}) %collective-permute-start.23) | collective-permute-done | bytes 32800 | tf_op jit(solution)/shard_map/ppermute | solution.py:301
  166.4 6.1 %collective-permute-done.24 = f32[16,512]{1,0:T(8,128)S(1)} collective-permute-done((f32[16,512]{1,0:T(8,128)S(1)}, f32[16,512]{1,0:T(8,128)S(1)}, u32[]{:S(2)}, u32[]{:S(2)}) %collective-permute-start.24) | collective-permute-done | bytes 32800 | tf_op jit(solution)/shard_map/ppermute | solution.py:301
  172.5 3.8 %collective-permute-start.25 = (f32[16,512]{1,0:T(8,128)S(1)}, f32[16,512]{1,0:T(8,128)S(1)}, u32[]{:S(2)}, u32[]{:S(2)}) collective-permute-start(f32[16,512]{1,0:T(8,128)S(1)} %get-tuple-element.26), channel_id=1, source_target_pairs={{0,4},{1,5},{2,6},{3,7},{4,8},{5,9},{6,10},{7,11},{8,12},{9,13},{1... | collective-permute-start | bytes 98312 | tf_op jit(solution)/shard_map/ppermute | solution.py:301
  177.1 6.0 %collective-permute-done.25 = f32[16,512]{1,0:T(8,128)S(1)} collective-permute-done((f32[16,512]{1,0:T(8,128)S(1)}, f32[16,512]{1,0:T(8,128)S(1)}, u32[]{:S(2)}, u32[]{:S(2)}) %collective-permute-start.25) | collective-permute-done | bytes 32800 | tf_op jit(solution)/shard_map/ppermute | solution.py:301
  186.2 9.2 %query.1.fq_ref = f32[768,512]{1,0:T(8,128)S(1)} custom-call(s32[3]{0:T(128)S(1)} %pad_add_fusion.place, bf16[768,4096]{1,0:T(8,128)(2,1)} %tok_hbm.3, bf16[16,4096]{1,0:T(8,128)(2,1)} %collective-permute-done.halo_hbm, bf16[2,512,512]{2,1,0:T(8,128)(2,1)S(1)} %pad_maximum_fusion.7.refs_0_, bf16[2,512,512]{2,1,0:T(8,128)(2,1)} %collective-permute-done.30.refs_1_, ...), custom_call_target="tpu_custom_call" | custom-call | flops 6442450944 | bytes 10485760 | tf_op jit(solution)/shard_map/query/pallas_call | solution.py:208
  195.4 6.5 %gate.1.own = bf16[768,512]{1,0:T(8,128)(2,1)S(1)} custom-call(f32[4,96,8,128]{3,2,1,0:T(8,128)S(1)} %copy-done, f32[16,8,512]{2,1,0:T(8,128)S(1)} %copy-done.16, f32[16,512]{1,0:T(8,128)S(1)} %multiply_add_fusion.enter_ref, f32[768,512]{1,0:T(8,128)S(1)} %query.1.fq_ref, f32[96,8,128]{2,1,0:T(8,128)S(1)} %broadcast_bitcast_fusion.keep_ref, ...), custom_call_target="tpu_custom_call" | custom-call | flops 31457280 | bytes 3932160 | tf_op jit(solution)/shard_map/gate/pallas_call | solution.py:231
  202.2 3.9 %dynamic-slice_bitcast_fusion = (bf16[1,512,1024]{2,1,0:T(8,128)(2,1)S(1)}, bf16[512,1024]{1,0:T(8,128)(2,1)}, bf16[512,1024]{1,0:T(8,128)(2,1)}, bf16[512,1024]{1,0:T(8,128)(2,1)}) fusion(bf16[512,4096]{1,0:T(8,128)(2,1)} %param.12, s32[]{:T(128)S(6)} %select_n.148, s32[]{:T(128)S(6)} %select_n.150, s32[]{:T(128)S(6)} %select_n.154, s32[]{:T(128)S(6)} %select_n.152), kind=kLoop, calls=%fused_computation.8 | loop fusion | bytes 8388624 | tf_op jit(solution)/shard_map/stack | solution.py:420
  206.0 3.0 %collective-permute-start.42 = (bf16[512,1024]{1,0:T(8,128)(2,1)}, bf16[512,1024]{1,0:T(8,128)(2,1)}, u32[]{:S(2)}, u32[]{:S(2)}) collective-permute-start(bf16[512,1024]{1,0:T(8,128)(2,1)} %get-tuple-element.19), channel_id=1, source_target_pairs={{0,192},{32,224},{64,0},{96,32},{128,64},{160,96},{192,128},{224,1... | collective-permute-start | bytes 3145736 | tf_op jit(solution)/shard_map/ppermute | solution.py:301
  214.0 41.4 %collective-permute-done.42 = bf16[512,1024]{1,0:T(8,128)(2,1)} collective-permute-done((bf16[512,1024]{1,0:T(8,128)(2,1)}, bf16[512,1024]{1,0:T(8,128)(2,1)}, u32[]{:S(2)}, u32[]{:S(2)}) %collective-permute-start.42) | collective-permute-done | bytes 1048608 | tf_op jit(solution)/shard_map/ppermute | solution.py:301
  255.4 3.2 %collective-permute-done.40 = bf16[512,1024]{1,0:T(8,128)(2,1)} collective-permute-done((bf16[512,1024]{1,0:T(8,128)(2,1)}, bf16[512,1024]{1,0:T(8,128)(2,1)}, u32[]{:S(2)}, u32[]{:S(2)}) %collective-permute-start.40) | collective-permute-done | bytes 1048608 | tf_op jit(solution)/shard_map/ppermute | solution.py:301
  262.5 12.9 %collective-permute-done.36.near = bf16[2,768,512]{2,1,0:T(8,128)(2,1)} collective-permute-done((bf16[2,768,512]{2,1,0:T(8,128)(2,1)}, bf16[2,768,512]{2,1,0:T(8,128)(2,1)}, u32[]{:S(2)}, u32[]{:S(2)}) %collective-permute-start.36) | collective-permute-done | bytes 1572896 | tf_op jit(solution)/shard_map/ppermute | solution.py:301
  276.6 13.2 %collective-permute-done.38.mid_own = bf16[2,384,512]{2,1,0:T(8,128)(2,1)S(1)} collective-permute-done((bf16[2,384,512]{2,1,0:T(8,128)(2,1)S(1)}, bf16[2,384,512]{2,1,0:T(8,128)(2,1)S(1)}, u32[]{:S(2)}, u32[]{:S(2)}) %collective-permute-start.38) | collective-permute-done | bytes 786464 | tf_op jit(solution)/shard_map/ppermute | solution.py:301
  293.3 6.5 %mix.1 = bf16[768,512]{1,0:T(8,128)(2,1)} custom-call(s32[3]{0:T(128)S(1)} %pad_add_fusion.place, bf16[768,512]{1,0:T(8,128)(2,1)S(1)} %gate.1.own, bf16[768,512]{1,0:T(8,128)(2,1)S(1)} %copy-done.4, bf16[2,768,512]{2,1,0:T(8,128)(2,1)} %collective-permute-done.36.near, bf16[2,768,512]{2,1,0:T(8,128)(2,1)S(1)} %collective-permute-done.37.far, ...), custom_call_target="tpu_custom_call" | custom-call | flops 3221225472 | bytes 10485760 | tf_op jit(solution)/shard_map/mix/pallas_call | solution.py:289
  (226 shorter events, 93.0 us)
Async XLA Ops:
  10.0 13.2 %collective-permute-start.9 = (bf16[2,128,1024]{2,1,0:T(8,128)(2,1)S(1)}, bf16[2,128,1024]{2,1,0:T(8,128)(2,1)S(1)}, u32[]{:S(2)}, u32[]{:S(2)}) collective-permute-start(bf16[2,128,1024]{2,1,0:T(8,128)(2,1)S(1)} %pad_maximum_fusion.10), channel_id=1, source_target_pairs={{0,8},{1,9},{2,10},{3,11},{4,12},{5,13},{6,14},{7,15},{8,16},{9,17... | collective-permute-start | bytes 1572872 | tf_op jit(solution)/shard_map/ppermute | solution.py:301
  32.1 16.9 %collective-permute-start.3 = (bf16[2,128,1024]{2,1,0:T(8,128)(2,1)}, bf16[2,128,1024]{2,1,0:T(8,128)(2,1)S(1)}, u32[]{:S(2)}, u32[]{:S(2)}) collective-permute-start(bf16[2,128,1024]{2,1,0:T(8,128)(2,1)} %collective-permute-done.2.refs_1_), channel_id=1, source_target_pairs={{0,32},{32,0},{64,96},{96,64},{128,160},{160,128},{192,224},{224,1... | collective-permute-start | bytes 1572872 | tf_op jit(solution)/shard_map/ppermute | solution.py:301
  36.5 28.5 %collective-permute-start.30 = (bf16[2,512,512]{2,1,0:T(8,128)(2,1)S(1)}, bf16[2,512,512]{2,1,0:T(8,128)(2,1)}, u32[]{:S(2)}, u32[]{:S(2)}) collective-permute-start(bf16[2,512,512]{2,1,0:T(8,128)(2,1)S(1)} %pad_maximum_fusion.7.refs_0_), channel_id=1, source_target_pairs={{0,1},{1,2},{2,3},{3,4},{4,5},{5,6},{6,7},{7,0},{8,9},{9,10},{10,1... | collective-permute-start | bytes 3145736 | tf_op jit(solution)/shard_map/ppermute | solution.py:301
  42.6 13.3 %collective-permute-start.7 = (bf16[2,64,1024]{2,1,0:T(8,128)(2,1)}, bf16[2,64,1024]{2,1,0:T(8,128)(2,1)S(1)}, u32[]{:S(2)}, u32[]{:S(2)}) collective-permute-start(bf16[2,64,1024]{2,1,0:T(8,128)(2,1)} %constant_dynamic-slice_fusion.10), channel_id=1, source_target_pairs={{0,1},{1,2},{2,3},{3,4},{4,5},{5,6},{6,7},{7,0},{8,9},{9,10},{10,1... | collective-permute-start | bytes 786440 | tf_op jit(solution)/shard_map/ppermute | solution.py:301
  44.6 17.0 %collective-permute-start.15 = (bf16[2,128,1024]{2,1,0:T(8,128)(2,1)}, bf16[2,128,1024]{2,1,0:T(8,128)(2,1)}, u32[]{:S(2)}, u32[]{:S(2)}) collective-permute-start(bf16[2,128,1024]{2,1,0:T(8,128)(2,1)} %maximum_select_fusion.1.refs_12_), channel_id=1, source_target_pairs={{0,1},{1,2},{2,3},{3,4},{4,5},{5,6},{6,7},{7,0},{8,9},{9,10},{10,1... | collective-permute-start | bytes 1572872 | tf_op jit(solution)/shard_map/ppermute | solution.py:301
  52.2 28.7 %collective-permute-start.10 = (bf16[2,256,1024]{2,1,0:T(8,128)(2,1)}, bf16[2,256,1024]{2,1,0:T(8,128)(2,1)}, u32[]{:S(2)}, u32[]{:S(2)}) collective-permute-start(bf16[2,256,1024]{2,1,0:T(8,128)(2,1)} %pad_maximum_fusion.5), channel_id=1, source_target_pairs={{0,8},{1,9},{2,10},{3,11},{4,12},{5,13},{6,14},{7,15},{8,16},{9,17... | collective-permute-start | bytes 3145736 | tf_op jit(solution)/shard_map/ppermute | solution.py:301
  56.8 18.1 %collective-permute-start.8 = (bf16[2,192,1024]{2,1,0:T(8,128)(2,1)}, bf16[2,192,1024]{2,1,0:T(8,128)(2,1)S(1)}, u32[]{:S(2)}, u32[]{:S(2)}) collective-permute-start(bf16[2,192,1024]{2,1,0:T(8,128)(2,1)} %pad_maximum_fusion.9), channel_id=1, source_target_pairs={{0,32},{32,0},{64,96},{96,64},{128,160},{160,128},{192,224},{224,1... | collective-permute-start | bytes 2359304 | tf_op jit(solution)/shard_map/ppermute | solution.py:301
  63.8 29.3 %collective-permute-start.11 = (bf16[2,256,1024]{2,1,0:T(8,128)(2,1)}, bf16[2,256,1024]{2,1,0:T(8,128)(2,1)}, u32[]{:S(2)}, u32[]{:S(2)}) collective-permute-start(bf16[2,256,1024]{2,1,0:T(8,128)(2,1)} %pad_maximum_fusion.6), channel_id=1, source_target_pairs={{0,8},{1,9},{2,10},{3,11},{4,12},{5,13},{6,14},{7,15},{8,16},{9,17... | collective-permute-start | bytes 3145736 | tf_op jit(solution)/shard_map/ppermute | solution.py:301
  65.0 20.0 %collective-permute-start.31 = (bf16[2,512,512]{2,1,0:T(8,128)(2,1)}, bf16[2,512,512]{2,1,0:T(8,128)(2,1)}, u32[]{:S(2)}, u32[]{:S(2)}) collective-permute-start(bf16[2,512,512]{2,1,0:T(8,128)(2,1)} %collective-permute-done.30.refs_1_), channel_id=1, source_target_pairs={{0,1},{1,2},{2,3},{3,4},{4,5},{5,6},{6,7},{7,0},{8,9},{9,10},{10,1... | collective-permute-start | bytes 3145736 | tf_op jit(solution)/shard_map/ppermute | solution.py:301
  72.3 56.4 %collective-permute-start = (bf16[16,4096]{1,0:T(8,128)(2,1)}, bf16[16,4096]{1,0:T(8,128)(2,1)}, u32[]{:S(2)}, u32[]{:S(2)}) collective-permute-start(bf16[16,4096]{1,0:T(8,128)(2,1)} %slice.78), channel_id=1, source_target_pairs={{0,1},{1,2},{2,3},{3,4},{4,5},{5,6},{6,7},{7,8},{8,9},{9,10},{10,1... | collective-permute-start | bytes 393224 | tf_op jit(solution)/shard_map/ppermute | solution.py:301
  75.0 17.0 %collective-permute-start.17 = (bf16[2,128,1024]{2,1,0:T(8,128)(2,1)}, bf16[2,128,1024]{2,1,0:T(8,128)(2,1)}, u32[]{:S(2)}, u32[]{:S(2)}) collective-permute-start(bf16[2,128,1024]{2,1,0:T(8,128)(2,1)} %collective-permute-done.16.refs_14_), channel_id=1, source_target_pairs={{0,1},{1,2},{2,3},{3,4},{4,5},{5,6},{6,7},{7,0},{8,9},{9,10},{10,1... | collective-permute-start | bytes 1572872 | tf_op jit(solution)/shard_map/ppermute | solution.py:301
  80.8 25.5 %collective-permute-start.12 = (bf16[2,384,1024]{2,1,0:T(8,128)(2,1)S(1)}, bf16[2,384,1024]{2,1,0:T(8,128)(2,1)S(1)}, u32[]{:S(2)}, u32[]{:S(2)}) collective-permute-start(bf16[2,384,1024]{2,1,0:T(8,128)(2,1)S(1)} %pad_maximum_fusion.2), channel_id=1, source_target_pairs={{0,8},{1,9},{2,10},{3,11},{4,12},{5,13},{6,14},{7,15},{8,16},{9,17... | collective-permute-start | bytes 4718600 | tf_op jit(solution)/shard_map/ppermute | solution.py:301
  85.0 21.2 %collective-permute-start.32 = (bf16[2,512,512]{2,1,0:T(8,128)(2,1)}, bf16[2,512,512]{2,1,0:T(8,128)(2,1)S(1)}, u32[]{:S(2)}, u32[]{:S(2)}) collective-permute-start(bf16[2,512,512]{2,1,0:T(8,128)(2,1)} %collective-permute-done.31.refs_2_), channel_id=1, source_target_pairs={{0,1},{1,2},{2,3},{3,4},{4,5},{5,6},{6,7},{7,0},{8,9},{9,10},{10,1... | collective-permute-start | bytes 3145736 | tf_op jit(solution)/shard_map/ppermute | solution.py:301
  94.3 34.5 %collective-permute-start.20 = (bf16[640,1024]{1,0:T(8,128)(2,1)S(1)}, bf16[640,1024]{1,0:T(8,128)(2,1)S(1)}, u32[]{:S(2)}, u32[]{:S(2)}) collective-permute-start(bf16[640,1024]{1,0:T(8,128)(2,1)S(1)} %pad_maximum_fusion.4), channel_id=1, source_target_pairs={{0,32},{32,0},{64,96},{96,64},{128,160},{160,128},{192,224},{224,1... | collective-permute-start | bytes 3932168 | tf_op jit(solution)/shard_map/ppermute | solution.py:301
  106.0 22.7 %collective-permute-start.19 = (bf16[448,1024]{1,0:T(8,128)(2,1)S(1)}, bf16[448,1024]{1,0:T(8,128)(2,1)S(1)}, u32[]{:S(2)}, u32[]{:S(2)}) collective-permute-start(bf16[448,1024]{1,0:T(8,128)(2,1)S(1)} %pad_maximum_fusion.8), channel_id=1, source_target_pairs={{0,32},{32,0},{64,96},{96,64},{128,160},{160,128},{192,224},{224,1... | collective-permute-start | bytes 2752520 | tf_op jit(solution)/shard_map/ppermute | solution.py:301
  106.4 22.4 %collective-permute-start.21 = (bf16[384,1024]{1,0:T(8,128)(2,1)S(1)}, bf16[384,1024]{1,0:T(8,128)(2,1)S(1)}, u32[]{:S(2)}, u32[]{:S(2)}) collective-permute-start(bf16[384,1024]{1,0:T(8,128)(2,1)S(1)} %slice_bitcast_fusion), channel_id=1, source_target_pairs={{0,32},{32,0},{64,96},{96,64},{128,160},{160,128},{192,224},{224,1... | collective-permute-start | bytes 2359304 | tf_op jit(solution)/shard_map/ppermute | solution.py:301
  119.0 64.2 %collective-permute-start.34 = (bf16[1792,512]{1,0:T(8,128)(2,1)}, bf16[1792,512]{1,0:T(8,128)(2,1)}, u32[]{:S(2)}, u32[]{:S(2)}) collective-permute-start(bf16[1792,512]{1,0:T(8,128)(2,1)} %pad_maximum_fusion.1), channel_id=1, source_target_pairs={{0,32},{32,0},{64,96},{96,64},{128,160},{160,128},{192,224},{224,1... | collective-permute-start | bytes 5505032 | tf_op jit(solution)/shard_map/ppermute | solution.py:301
  206.0 49.3 %collective-permute-start.42 = (bf16[512,1024]{1,0:T(8,128)(2,1)}, bf16[512,1024]{1,0:T(8,128)(2,1)}, u32[]{:S(2)}, u32[]{:S(2)}) collective-permute-start(bf16[512,1024]{1,0:T(8,128)(2,1)} %get-tuple-element.19), channel_id=1, source_target_pairs={{0,192},{32,224},{64,0},{96,32},{128,64},{160,96},{192,128},{224,1... | collective-permute-start | bytes 3145736 | tf_op jit(solution)/shard_map/ppermute | solution.py:301
  209.1 46.3 %collective-permute-start.41 = (bf16[512,1024]{1,0:T(8,128)(2,1)}, bf16[512,1024]{1,0:T(8,128)(2,1)}, u32[]{:S(2)}, u32[]{:S(2)}) collective-permute-start(bf16[512,1024]{1,0:T(8,128)(2,1)} %get-tuple-element.20), channel_id=1, source_target_pairs={{0,128},{32,160},{64,192},{96,224},{128,0},{160,32},{192,64},{224,... | collective-permute-start | bytes 3145736 | tf_op jit(solution)/shard_map/ppermute | solution.py:301
  209.7 48.8 %collective-permute-start.40 = (bf16[512,1024]{1,0:T(8,128)(2,1)}, bf16[512,1024]{1,0:T(8,128)(2,1)}, u32[]{:S(2)}, u32[]{:S(2)}) collective-permute-start(bf16[512,1024]{1,0:T(8,128)(2,1)} %get-tuple-element.18), channel_id=1, source_target_pairs={{0,64},{32,96},{64,128},{96,160},{128,192},{160,224},{192,0},{224,... | collective-permute-start | bytes 3145736 | tf_op jit(solution)/shard_map/ppermute | solution.py:301
  212.1 63.3 %collective-permute-start.36 = (bf16[2,768,512]{2,1,0:T(8,128)(2,1)}, bf16[2,768,512]{2,1,0:T(8,128)(2,1)}, u32[]{:S(2)}, u32[]{:S(2)}) collective-permute-start(bf16[2,768,512]{2,1,0:T(8,128)(2,1)} %pad_maximum_fusion.3), channel_id=1, source_target_pairs={{0,64},{32,224},{64,128},{96,32},{128,192},{160,96},{192,0},{224,1... | collective-permute-start | bytes 4718600 | tf_op jit(solution)/shard_map/ppermute | solution.py:301
  262.5 27.3 %collective-permute-start.43 = (bf16[4,512,512]{2,1,0:T(8,128)(2,1)}, bf16[4,512,512]{2,1,0:T(8,128)(2,1)}, u32[]{:S(2)}, u32[]{:S(2)}) collective-permute-start(bf16[4,512,512]{2,1,0:T(8,128)(2,1)} %get-tuple-element.15), channel_id=1, source_target_pairs={{0,32},{32,0},{64,96},{96,64},{128,160},{160,128},{192,224},{224,1... | collective-permute-start | bytes 6291464 | tf_op jit(solution)/shard_map/ppermute | solution.py:301
  275.4 14.5 %collective-permute-start.37 = (bf16[2,768,512]{2,1,0:T(8,128)(2,1)}, bf16[2,768,512]{2,1,0:T(8,128)(2,1)S(1)}, u32[]{:S(2)}, u32[]{:S(2)}) collective-permute-start(bf16[2,768,512]{2,1,0:T(8,128)(2,1)} %collective-permute-done.36.near), channel_id=1, source_target_pairs={{0,32},{32,0},{64,96},{96,64},{128,160},{160,128},{192,224},{224,1... | collective-permute-start | bytes 4718600 | tf_op jit(solution)/shard_map/ppermute | solution.py:301
  276.6 13.3 %collective-permute-start.38 = (bf16[2,384,512]{2,1,0:T(8,128)(2,1)S(1)}, bf16[2,384,512]{2,1,0:T(8,128)(2,1)S(1)}, u32[]{:S(2)}, u32[]{:S(2)}) collective-permute-start(bf16[2,384,512]{2,1,0:T(8,128)(2,1)S(1)} %constant_dynamic-slice_fusion.5), channel_id=1, source_target_pairs={{0,64},{32,224},{64,128},{96,32},{128,192},{160,96},{192,0},{224,1... | collective-permute-start | bytes 2359304 | tf_op jit(solution)/shard_map/ppermute | solution.py:301
  (57 other events, 626.0 us)
